TPU v7x, 32 devices: a whole 2x2x4 slice. The times are simulated.
32 devices in a mesh: dp: 4 (over y, x), mp: 8 (over z, core).
Axes of the slice: x: 2, y: 2, z: 4, core: 2. Of those that a mesh axis runs over, the one named last changes fastest.
Arguments:
- hidden_in: bfloat16 [8192, 2048], P(('dp', 'mp')), may hold values from -6 to 6
- cotangent: bfloat16 [8192, 2048], P(('dp', 'mp')), may hold values from -6 to 6
- domain_tags: int32 [4], P('dp'), may hold values from 0 to 2
- mix_weight: bfloat16 [2, 2048, 3, 2048], P(None, None, None, 'mp'), may hold values from -0.125 to 0.125
- mix_out_weight: bfloat16 [2, 2048, 2048], P(None, 'mp'), may hold values from -0.125 to 0.125
- glu_weight: bfloat16 [2, 2048, 2, 5632], P(None, None, None, 'mp'), may hold values from -0.125 to 0.125
- glu_out_weight: bfloat16 [2, 5632, 2048], P(None, 'mp'), may hold values from -0.078125 to 0.078125
- mix_gain: float32 [2, 2048], replicated, may hold values from 0.5 to 1.5
- out_gain: float32 [2, 2048], P(None, 'mp'), may hold values from 0.5 to 1.5
- glu_gain: float32 [2, 2048], replicated, may hold values from 0.5 to 1.5
- bound_logits: float32 [3, 2048], P(None, 'mp'), may hold values from -4 to 4
Outputs:
- hidden_out: float32 [8192, 2048], P(('dp', 'mp'))
- input_grad: float32 [8192, 2048], P(('dp', 'mp'))
- mix_weight_grad: float32 [2, 2048, 3, 2048], P(None, None, None, 'mp')
- mix_out_grad: float32 [2, 2048, 2048], P(None, 'mp')
- glu_weight_grad: float32 [2, 2048, 2, 5632], P(None, None, None, 'mp')
- glu_out_grad: float32 [2, 5632, 2048], P(None, 'mp')
- mix_gain_grad: float32 [2, 2048], replicated
- out_gain_grad: float32 [2, 2048], P(None, 'mp')
- glu_gain_grad: float32 [2, 2048], replicated
- bound_grad: float32 [3, 2048], P(None, 'mp')
All inputs are finite; a program needn't handle non-finite values.
Results may differ from a plain program's by a relative error of at most 0.034.
Values may be sent and summed in bfloat16 or wider, within the bound.
No kernel may reach another device: no remote copies, remote signals or barrier semaphores. Data moves between devices by JAX's collectives and lax.ppermute only.
A program may use at most 384 MiB of HBM per device.

v0:
```python
import jax
import jax.numpy as jnp
from jax import lax
from jax.sharding import PartitionSpec as P

norm_eps = 1e-06
domain_scale = (1.0, 0.5, 2.0)


def scaled_rms(values, gain_vec):
    return values * lax.rsqrt(jnp.mean(values * values, -1, keepdims=True) + norm_eps) * gain_vec


def bound_rows(logits):
    return jnp.cumsum(jax.nn.softmax(logits, 0), 0)


def recurrence(projected, lower_bound, seq_count):
    inputs = projected[:, 0]
    forget_pre = projected[:, 1]
    gate_pre = projected[:, 2]
    forget = lower_bound + (1.0 - lower_bound) * jax.nn.sigmoid(forget_pre)
    update = (1.0 - forget) * jax.nn.silu(inputs)
    seq_shape = (seq_count, -1, projected.shape[2])

    def combine(earlier, later_part):
        return (earlier[0] * later_part[0], later_part[0] * earlier[1] + later_part[1])

    scanned = lax.associative_scan(
        combine, (forget.reshape(seq_shape), update.reshape(seq_shape)), axis=1
    )
    return scanned[1].reshape(update.shape) * jax.nn.silu(gate_pre)


def inner_terms(projected, lower_bound, seq_count):
    gate_out = recurrence(projected, lower_bound, seq_count)
    return (gate_out, jnp.sum(gate_out * gate_out, -1))


def gate_norm(gate_out, square_total, gain_vec, width_full):
    return gate_out * lax.rsqrt(square_total / width_full + norm_eps)[:, None] * gain_vec


def glu_act(gate_up):
    return jax.nn.silu(gate_up[:, 0]) * gate_up[:, 1]


def local(
    hidden_in,
    cotangent,
    domain_tags,
    mix_weight,
    mix_out_weight,
    glu_weight,
    glu_out_weight,
    mix_gain,
    out_gain,
    glu_gain,
    bound_logits,
):
    local_rows = hidden_in.shape[0]
    width_full = hidden_in.shape[1]
    group_rows = local_rows * lax.axis_size("mp")
    seq_count = domain_tags.shape[0]
    seq_length = group_rows // seq_count
    layer_count = mix_weight.shape[0]
    channels = mix_weight.shape[3]
    hidden_units = glu_weight.shape[3]
    bound_vals, bound_back = jax.vjp(bound_rows, bound_logits)
    stream = hidden_in.astype(jnp.float32)
    kept_values = []
    for layer_index in range(layer_count):
        normed, mix_norm_back = jax.vjp(scaled_rms, stream, mix_gain[layer_index])
        mixer_in = lax.all_gather(normed.astype(jnp.bfloat16), "mp", axis=0, tiled=True)
        projected = jnp.dot(
            mixer_in,
            mix_weight[layer_index].reshape(width_full, 3 * channels),
            preferred_element_type=jnp.float32,
        ).reshape(group_rows, 3, channels)
        (gate_out, square_part), inner_back = jax.vjp(
            lambda proj_in, bound_in: inner_terms(proj_in, bound_in, seq_count),
            projected,
            bound_vals[layer_index],
        )
        square_total = lax.psum(square_part, "mp")
        mixed, outer_back = jax.vjp(
            lambda gated_in, total_in, gain_in: gate_norm(gated_in, total_in, gain_in, width_full),
            gate_out,
            square_total,
            out_gain[layer_index],
        )
        mixed_low = mixed.astype(jnp.bfloat16)

        def out_rows(row_start, row_count, source=mixed_low, matrix=mix_out_weight[layer_index]):
            return jnp.dot(source, matrix, preferred_element_type=jnp.float32)

        stream_mid = stream + lax.psum_scatter(
            out_rows(jnp.int32(0), local_rows * lax.axis_size("mp")).astype(jnp.bfloat16),
            "mp",
            scatter_dimension=0,
            tiled=True,
        ).astype(jnp.float32)
        glu_normed, glu_norm_back = jax.vjp(scaled_rms, stream_mid, glu_gain[layer_index])
        glu_in = lax.all_gather(glu_normed.astype(jnp.bfloat16), "mp", axis=0, tiled=True)
        gate_up = jnp.dot(
            glu_in,
            glu_weight[layer_index].reshape(width_full, 2 * hidden_units),
            preferred_element_type=jnp.float32,
        ).reshape(group_rows, 2, hidden_units)
        hidden_val, act_back = jax.vjp(glu_act, gate_up)
        hidden_low = hidden_val.astype(jnp.bfloat16)

        def down_rows(row_start, row_count, source=hidden_low, matrix=glu_out_weight[layer_index]):
            return jnp.dot(source, matrix, preferred_element_type=jnp.float32)

        stream = stream_mid + lax.psum_scatter(
            down_rows(jnp.int32(0), local_rows * lax.axis_size("mp")).astype(jnp.bfloat16),
            "mp",
            scatter_dimension=0,
            tiled=True,
        ).astype(jnp.float32)
        kept_values.append(
            (
                mix_norm_back,
                mixer_in,
                inner_back,
                outer_back,
                mixed_low,
                glu_norm_back,
                glu_in,
                act_back,
                hidden_low,
            )
        )
    row_index = lax.axis_index("mp") * local_rows + jnp.arange(local_rows, dtype=jnp.int32)
    seq_index = row_index // seq_length
    seq_match = seq_index[:, None] == jnp.arange(seq_count, dtype=jnp.int32)[None, :]
    row_tags = jnp.sum(jnp.where(seq_match, domain_tags[None, :], 0), -1)
    scale_table = jnp.array(domain_scale, dtype=jnp.float32)
    tag_match = row_tags[:, None] == jnp.arange(3, dtype=jnp.int32)[None, :]
    row_scale = jnp.sum(jnp.where(tag_match, scale_table[None, :], 0.0), -1)
    grad_stream = cotangent.astype(jnp.float32) * row_scale[:, None]
    mix_grads = [None] * layer_count
    mix_out_grads = [None] * layer_count
    glu_grads = [None] * layer_count
    glu_out_grads = [None] * layer_count
    out_gain_parts = [None] * layer_count
    bound_parts = [None] * layer_count
    mix_gain_parts = [None] * layer_count
    glu_gain_parts = [None] * layer_count
    for layer_index in reversed(range(layer_count)):
        (
            mix_norm_back,
            mixer_in,
            inner_back,
            outer_back,
            mixed_low,
            glu_norm_back,
            glu_in,
            act_back,
            hidden_low,
        ) = kept_values[layer_index]
        down_grad = lax.all_gather(grad_stream.astype(jnp.bfloat16), "mp", axis=0, tiled=True)
        glu_out_grads[layer_index] = jnp.einsum(
            "tf,td->fd", hidden_low, down_grad, preferred_element_type=jnp.float32
        )
        hidden_grad = jnp.einsum(
            "td,fd->tf", down_grad, glu_out_weight[layer_index], preferred_element_type=jnp.float32
        )
        gate_up_low = act_back(hidden_grad)[0].astype(jnp.bfloat16)
        glu_grads[layer_index] = jnp.einsum(
            "td,tkf->dkf", glu_in, gate_up_low, preferred_element_type=jnp.float32
        )

        def glu_back_rows(row_start, row_count, source=gate_up_low, matrix=glu_weight[layer_index]):
            return jnp.einsum("tkf,dkf->td", source, matrix, preferred_element_type=jnp.float32)

        input_part = lax.psum_scatter(
            glu_back_rows(jnp.int32(0), local_rows * lax.axis_size("mp")).astype(jnp.bfloat16),
            "mp",
            scatter_dimension=0,
            tiled=True,
        ).astype(jnp.float32)
        stream_part, glu_gain_parts[layer_index] = glu_norm_back(input_part)
        grad_stream = grad_stream + stream_part
        out_grad = lax.all_gather(grad_stream.astype(jnp.bfloat16), "mp", axis=0, tiled=True)
        mix_out_grads[layer_index] = jnp.einsum(
            "tc,td->cd", mixed_low, out_grad, preferred_element_type=jnp.float32
        )
        mixed_grad = jnp.einsum(
            "td,cd->tc", out_grad, mix_out_weight[layer_index], preferred_element_type=jnp.float32
        )
        gated_grad, total_grad, out_gain_parts[layer_index] = outer_back(mixed_grad)
        total_grad = lax.psum(total_grad, "mp")
        proj_grad, bound_parts[layer_index] = inner_back((gated_grad, total_grad))
        proj_low = proj_grad.astype(jnp.bfloat16)
        mix_grads[layer_index] = jnp.einsum(
            "td,tkc->dkc", mixer_in, proj_low, preferred_element_type=jnp.float32
        )

        def mix_back_rows(row_start, row_count, source=proj_low, matrix=mix_weight[layer_index]):
            return jnp.einsum("tkc,dkc->td", source, matrix, preferred_element_type=jnp.float32)

        input_part = lax.psum_scatter(
            mix_back_rows(jnp.int32(0), local_rows * lax.axis_size("mp")).astype(jnp.bfloat16),
            "mp",
            scatter_dimension=0,
            tiled=True,
        ).astype(jnp.float32)
        stream_part, mix_gain_parts[layer_index] = mix_norm_back(input_part)
        grad_stream = grad_stream + stream_part
    extra_rows = jnp.zeros((bound_vals.shape[0] - layer_count, channels), jnp.float32)
    bound_cot = jnp.concatenate([jnp.stack(bound_parts), extra_rows], 0)
    bound_local = bound_back(bound_cot)[0]
    mix_weight_grad, mix_out_grad, glu_weight_grad, glu_out_grad, out_gain_grad, bound_grad = (
        lax.psum(jnp.stack(mix_grads).astype(jnp.bfloat16), "dp").astype(jnp.float32),
        lax.psum(jnp.stack(mix_out_grads).astype(jnp.bfloat16), "dp").astype(jnp.float32),
        lax.psum(jnp.stack(glu_grads).astype(jnp.bfloat16), "dp").astype(jnp.float32),
        lax.psum(jnp.stack(glu_out_grads).astype(jnp.bfloat16), "dp").astype(jnp.float32),
        lax.psum(jnp.stack(out_gain_parts).astype(jnp.bfloat16), "dp").astype(jnp.float32),
        lax.psum(bound_local.astype(jnp.bfloat16), "dp").astype(jnp.float32),
    )
    mix_gain_grad, glu_gain_grad = lax.psum(
        (jnp.stack(mix_gain_parts), jnp.stack(glu_gain_parts)), ("dp", "mp")
    )
    return (
        stream,
        grad_stream,
        mix_weight_grad,
        mix_out_grad,
        glu_weight_grad,
        glu_out_grad,
        mix_gain_grad,
        out_gain_grad,
        glu_gain_grad,
        bound_grad,
    )


def solution(mesh):
    return jax.shard_map(
        local,
        mesh=mesh,
        in_specs=(
            P(("dp", "mp"), None),
            P(("dp", "mp"), None),
            P("dp"),
            P(None, None, None, "mp"),
            P(None, "mp", None),
            P(None, None, None, "mp"),
            P(None, "mp", None),
            P(),
            P(None, "mp"),
            P(),
            P(None, "mp"),
        ),
        out_specs=(
            P(("dp", "mp"), None),
            P(("dp", "mp"), None),
            P(None, None, None, "mp"),
            P(None, "mp", None),
            P(None, None, None, "mp"),
            P(None, "mp", None),
            P(),
            P(None, "mp"),
            P(),
            P(None, "mp"),
        ),
        check_vma=False,
    )
```

profile of v0, /device:TPU:0, one launch (start us, length us, event | category | flops | bytes accessed | tf_op | source)
XLA Modules:
  0.0 2793.3 jit_solution(14125348129023636350)
XLA Ops:
  25.3 72.9 %all-gather.9.cloned.1.call-done = bf16[2048,2048]{1,0:T(8,128)(2,1)} async-done(((bf16[256,2048]{1,0:T(8,128)(2,1)}), bf16[2048,2048]{1,0:T(8,128)(2,1)}) %all-gather.9.cloned.1.call-update) | async-done | bytes 8388624 | tf_op jit(solution)/shard_map/all_gather | solution.py:74
  203.6 23.8 psum.84
  237.9 86.9 %reduce-scatter.9.cloned.1.call-done = bf16[256,2048]{1,0:T(8,128)(2,1)} async-done(((bf16[2048,2048]{1,0:T(8,128)(2,1)}), bf16[256,2048]{1,0:T(8,128)(2,1)}) %reduce-scatter.9.cloned.1.call-update) | async-done | bytes 1048592 | tf_op jit(solution)/shard_map/reduce_scatter | solution.py:97
  328.1 80.5 %all-gather.11.cloned.1.call-done = bf16[2048,2048]{1,0:T(8,128)(2,1)} async-done(((bf16[256,2048]{1,0:T(8,128)(2,1)}), bf16[2048,2048]{1,0:T(8,128)(2,1)}) %all-gather.11.cloned.1.call-update) | async-done | bytes 8388624 | tf_op jit(solution)/shard_map/all_gather | solution.py:104
  408.6 16.6 fusion.10
  440.8 88.3 %reduce-scatter.11.cloned.1.call-done = bf16[256,2048]{1,0:T(8,128)(2,1)} async-done(((bf16[2048,2048]{1,0:T(8,128)(2,1)}), bf16[256,2048]{1,0:T(8,128)(2,1)}) %reduce-scatter.11.cloned.1.call-update) | async-done | bytes 1048592 | tf_op jit(solution)/shard_map/reduce_scatter | solution.py:116
  539.3 75.5 %all-gather.13.cloned.1.call-done = bf16[2048,2048]{1,0:T(8,128)(2,1)} async-done(((bf16[256,2048]{1,0:T(8,128)(2,1)}), bf16[2048,2048]{1,0:T(8,128)(2,1)}) %all-gather.13.cloned.1.call-update) | async-done | bytes 8388624 | tf_op jit(solution)/shard_map/all_gather | solution.py:74
  759.6 14.4 psum.85
  783.8 88.1 %reduce-scatter.13.cloned.1.call-done = bf16[256,2048]{1,0:T(8,128)(2,1)} async-done(((bf16[2048,2048]{1,0:T(8,128)(2,1)}), bf16[256,2048]{1,0:T(8,128)(2,1)}) %reduce-scatter.13.cloned.1.call-update) | async-done | bytes 1048592 | tf_op jit(solution)/shard_map/reduce_scatter | solution.py:97
  881.3 76.1 %all-gather.15.cloned.1.call-done = bf16[2048,2048]{1,0:T(8,128)(2,1)} async-done(((bf16[256,2048]{1,0:T(8,128)(2,1)}), bf16[2048,2048]{1,0:T(8,128)(2,1)}) %all-gather.15.cloned.1.call-update) | async-done | bytes 8388624 | tf_op jit(solution)/shard_map/all_gather | solution.py:104
  957.4 18.8 fusion.2
  976.2 64.0 %all-gather.17.cloned.1.call-done = bf16[2048,2048]{1,0:T(8,128)(2,1)} async-done(((bf16[256,2048]{1,0:T(8,128)(2,1)}), bf16[2048,2048]{1,0:T(8,128)(2,1)}) %all-gather.17.cloned.1.call-update) | async-done | bytes 8388624 | tf_op jit(solution)/shard_map/all_gather | solution.py:163
  1040.2 15.9 multiply_bitcast_fusion.1
  1058.6 19.3 bitcast_convert_fusion.3
  1078.0 88.2 %reduce-scatter.17.cloned.1.call-done = bf16[256,2048]{1,0:T(8,128)(2,1)} async-done(((bf16[2048,2048]{1,0:T(8,128)(2,1)}), bf16[256,2048]{1,0:T(8,128)(2,1)}) %reduce-scatter.17.cloned.1.call-update) | async-done | bytes 1048592 | tf_op jit(solution)/shard_map/reduce_scatter | solution.py:178
  1171.6 80.5 %all-gather.19.cloned.1.call-done = bf16[2048,2048]{1,0:T(8,128)(2,1)} async-done(((bf16[256,2048]{1,0:T(8,128)(2,1)}), bf16[2048,2048]{1,0:T(8,128)(2,1)}) %all-gather.19.cloned.1.call-update) | async-done | bytes 8388624 | tf_op jit(solution)/shard_map/all_gather | solution.py:186
  1261.7 15.3 psum.86
  1567.8 12.7 convolution_convert_fusion
  1580.7 75.2 %reduce-scatter.19.cloned.1.call-done = bf16[256,2048]{1,0:T(8,128)(2,1)} async-done(((bf16[2048,2048]{1,0:T(8,128)(2,1)}), bf16[256,2048]{1,0:T(8,128)(2,1)}) %reduce-scatter.19.cloned.1.call-update) | async-done | bytes 1048592 | tf_op jit(solution)/shard_map/reduce_scatter | solution.py:204
  1658.4 87.7 %reduce-scatter.15.cloned.1.call-done = bf16[256,2048]{1,0:T(8,128)(2,1)} async-done(((bf16[2048,2048]{1,0:T(8,128)(2,1)}), bf16[256,2048]{1,0:T(8,128)(2,1)}) %reduce-scatter.15.cloned.1.call-update) | async-done | bytes 1048592 | tf_op jit(solution)/shard_map/reduce_scatter | solution.py:116
  1751.1 80.5 %all-gather.21.cloned.1.call-done = bf16[2048,2048]{1,0:T(8,128)(2,1)} async-done(((bf16[256,2048]{1,0:T(8,128)(2,1)}), bf16[2048,2048]{1,0:T(8,128)(2,1)}) %all-gather.21.cloned.1.call-update) | async-done | bytes 8388624 | tf_op jit(solution)/shard_map/all_gather | solution.py:163
  1831.6 14.5 multiply_bitcast_fusion
  1850.4 17.4 bitcast_convert_fusion.1
  1867.8 88.2 %reduce-scatter.21.cloned.1.call-done = bf16[256,2048]{1,0:T(8,128)(2,1)} async-done(((bf16[2048,2048]{1,0:T(8,128)(2,1)}), bf16[256,2048]{1,0:T(8,128)(2,1)}) %reduce-scatter.21.cloned.1.call-update) | async-done | bytes 1048592 | tf_op jit(solution)/shard_map/reduce_scatter | solution.py:178
  1962.0 80.0 %all-gather.23.cloned.1.call-done = bf16[2048,2048]{1,0:T(8,128)(2,1)} async-done(((bf16[256,2048]{1,0:T(8,128)(2,1)}), bf16[2048,2048]{1,0:T(8,128)(2,1)}) %all-gather.23.cloned.1.call-update) | async-done | bytes 8388624 | tf_op jit(solution)/shard_map/all_gather | solution.py:186
  2051.1 14.3 psum.87
  2197.7 13.5 fusion.59
  2211.2 17.8 convert_bitcast_fusion
  2242.6 12.3 fusion.58
  2258.3 19.3 convert_bitcast_fusion.1
  2324.5 38.3 %all-reduce.220 = (f32[2,2048]{1,0:T(2,128)}, f32[2,2048]{1,0:T(2,128)}) all-reduce(f32[2,2048]{1,0:T(2,128)S(1)} %get-tuple-element.293, f32[2,2048]{1,0:T(2,128)S(1)} %get-tuple-element.294), channel_id=1, replica_groups=mesh['dp'=4,'mp'=8] {'dp','mp'}, use_global_device_ids=true, to_apply=%region_34.35 | all-reduce | flops 8192 | bytes 65536 | tf_op jit(solution)/shard_map/psum | solution.py:223
  2367.8 390.8 %all-reduce.225.cloned.1.call-done = (bf16[2,2048,3,256]{3,1,2,0:T(8,128)(2,1)}, bf16[2,256,2048]{2,1,0:T(8,128)(2,1)}, bf16[2,2048,2,704]{1,3,2,0:T(8,128)(2,1)}, bf16[2,704,2048]{2,1,0:T(8,128)(2,1)}) async-done(((bf16[2,2048,3,256]{3,1,2,0:T(8,128)(2,1)}, bf16[2,256,2048]{2,1,0:T(8,128)(2,1)}, bf16[2,2048,2,704]{1,3,2,0:T(8,128)(2,1)}, bf16[2,704,2048]{2,1,0:T(8,128)(2,1)}), ...) | async-done | bytes 25690128 | tf_op jit(solution)/shard_map/psum | solution.py:216
  (1307 shorter events, 885.9 us)
Async XLA Ops:
  7.2 91.0 %all-gather.9.cloned.1.call-start = ((), (), s32[]{:S(2)}) async-start(), calls=%async_computation.8 | async-start | bytes 9437184 | tf_op jit(solution)/shard_map/all_gather | solution.py:74
  13.3 311.5 %reduce-scatter.9.cloned.1.call-start = ((), (), s32[]{:S(2)}) async-start(), calls=%async_computation.9 | async-start | bytes 9437184 | tf_op jit(solution)/shard_map/reduce_scatter | solution.py:97
  24.0 84.2 %copy-start.252 = (f32[256]{0:T(256)}, f32[256]{0:T(256)S(1)}, u32[]{:S(2)}) copy-start(f32[256]{0:T(256)S(1)} %reduce_max.9) | copy-start | bytes 3076
  24.1 84.2 %copy-start.278 = (f32[256]{0:T(256)}, f32[256]{0:T(256)S(1)}, u32[]{:S(2)}) copy-start(f32[256]{0:T(256)S(1)} %fusion.235) | copy-start | bytes 3076
  25.3 83.0 %copy-start.285 = (f32[1,256]{1,0:T(1,128)}, f32[1,256]{1,0:T(1,128)S(1)}, u32[]{:S(2)}) copy-start(f32[1,256]{1,0:T(1,128)S(1)} %get-tuple-element.258) | copy-start | bytes 3076
  25.3 83.0 %copy-start.287 = (f32[1,256]{1,0:T(1,128)}, f32[1,256]{1,0:T(1,128)S(1)}, u32[]{:S(2)}) copy-start(f32[1,256]{1,0:T(1,128)S(1)} %get-tuple-element.260) | copy-start | bytes 3076
  236.6 88.2 %copy-start = (bf16[256,2048]{1,0:T(8,128)(2,1)S(1)}, bf16[256,2048]{1,0:T(8,128)(2,1)}, u32[]{:S(2)}) copy-start(bf16[256,2048]{1,0:T(8,128)(2,1)} %param.12) | copy-start | bytes 3145732
  236.6 172.0 %all-gather.11.cloned.1.call-start = ((), (), s32[]{:S(2)}) async-start(), calls=%async_computation.10 | async-start | bytes 9437184 | tf_op jit(solution)/shard_map/all_gather | solution.py:104
  237.9 90.1 %copy-start.186 = (f32[1,2048]{1,0:T(1,128)}, f32[1,2048]{1,0:T(1,128)S(1)}, u32[]{:S(2)}) copy-start(f32[1,2048]{1,0:T(1,128)S(1)} %get-tuple-element.223) | copy-start | bytes 24580
  328.1 200.9 %reduce-scatter.11.cloned.1.call-start = ((), (), s32[]{:S(2)}) async-start(), calls=%async_computation.11 | async-start | bytes 9437184 | tf_op jit(solution)/shard_map/reduce_scatter | solution.py:116
  440.7 174.1 %all-gather.13.cloned.1.call-start = ((), (), s32[]{:S(2)}) async-start(), calls=%async_computation.12 | async-start | bytes 9437184 | tf_op jit(solution)/shard_map/all_gather | solution.py:74
  534.2 337.7 %reduce-scatter.13.cloned.1.call-start = ((), (), s32[]{:S(2)}) async-start(), calls=%async_computation.13 | async-start | bytes 9437184 | tf_op jit(solution)/shard_map/reduce_scatter | solution.py:97
  783.8 173.6 %all-gather.15.cloned.1.call-start = ((), (), s32[]{:S(2)}) async-start(), calls=%async_computation.14 | async-start | bytes 9437184 | tf_op jit(solution)/shard_map/all_gather | solution.py:104
  876.8 163.4 %all-gather.17.cloned.1.call-start = ((), (), s32[]{:S(2)}) async-start(), calls=%async_computation.16 | async-start | bytes 9437184 | tf_op jit(solution)/shard_map/all_gather | solution.py:163
  881.3 285.0 %reduce-scatter.17.cloned.1.call-start = ((), (), s32[]{:S(2)}) async-start(), calls=%async_computation.17 | async-start | bytes 9437184 | tf_op jit(solution)/shard_map/reduce_scatter | solution.py:178
  1077.9 174.2 %all-gather.19.cloned.1.call-start = ((), (), s32[]{:S(2)}) async-start(), calls=%async_computation.18 | async-start | bytes 9437184 | tf_op jit(solution)/shard_map/all_gather | solution.py:186
  1171.5 484.4 %reduce-scatter.19.cloned.1.call-start = ((), (), s32[]{:S(2)}) async-start(), calls=%async_computation.19 | async-start | bytes 9437184 | tf_op jit(solution)/shard_map/reduce_scatter | solution.py:204
  1567.8 178.3 %reduce-scatter.15.cloned.1.call-start = ((), (), s32[]{:S(2)}) async-start(), calls=%async_computation.15 | async-start | bytes 9437184 | tf_op jit(solution)/shard_map/reduce_scatter | solution.py:116
  1580.6 165.5 %copy-start.185 = (f32[1,2048]{1,0:T(1,128)S(1)}, f32[1,2048]{1,0:T(1,128)}, u32[]{:S(2)}) copy-start(f32[1,2048]{1,0:T(1,128)} %get-tuple-element.224) | copy-start | bytes 24580
  1580.6 165.5 %copy-start.256 = (f32[256]{0:T(256)S(1)}, f32[256]{0:T(256)}, u32[]{:S(2)}) copy-start(f32[256]{0:T(256)} %copy-done.254) | copy-start | bytes 3076
  1580.6 165.5 %copy-start.270 = (f32[256]{0:T(256)S(1)}, f32[256]{0:T(256)}, u32[]{:S(2)}) copy-start(f32[256]{0:T(256)} %copy-done.268) | copy-start | bytes 3076
  1580.6 165.5 %copy-start.284 = (f32[256]{0:T(256)S(1)}, f32[256]{0:T(256)}, u32[]{:S(2)}) copy-start(f32[256]{0:T(256)} %copy-done.283) | copy-start | bytes 3076
  1580.6 251.0 %all-gather.21.cloned.1.call-start = ((), (), s32[]{:S(2)}) async-start(), calls=%async_computation.20 | async-start | bytes 9437184 | tf_op jit(solution)/shard_map/all_gather | solution.py:163
  1751.0 205.1 %reduce-scatter.21.cloned.1.call-start = ((), (), s32[]{:S(2)}) async-start(), calls=%async_computation.21 | async-start | bytes 9437184 | tf_op jit(solution)/shard_map/reduce_scatter | solution.py:178
  1867.7 88.3 %copy-start.1 = (bf16[256,2048]{1,0:T(8,128)(2,1)S(1)}, bf16[256,2048]{1,0:T(8,128)(2,1)}, u32[]{:S(2)}) copy-start(bf16[256,2048]{1,0:T(8,128)(2,1)} %param.12) | copy-start | bytes 3145732
  1867.8 88.3 %copy-start.6 = (bf16[256,2048]{1,0:T(8,128)(2,1)S(1)}, bf16[256,2048]{1,0:T(8,128)(2,1)}, u32[]{:S(2)}) copy-start(bf16[256,2048]{1,0:T(8,128)(2,1)} %reduce-scatter.9.cloned.1.call-done) | copy-start | bytes 3145732
  1867.8 88.3 %copy-start.187 = (f32[1,2048]{1,0:T(1,128)S(1)}, f32[1,2048]{1,0:T(1,128)}, u32[]{:S(2)}) copy-start(f32[1,2048]{1,0:T(1,128)} %copy-done.186) | copy-start | bytes 24580
  1867.8 88.3 %copy-start.258 = (f32[256]{0:T(256)S(1)}, f32[256]{0:T(256)}, u32[]{:S(2)}) copy-start(f32[256]{0:T(256)} %copy-done.257) | copy-start | bytes 3076
  1867.8 91.3 %copy-start.292 = (f32[256]{0:T(256)S(1)}, f32[256]{0:T(256)}, u32[]{:S(2)}) copy-start(f32[256]{0:T(256)} %copy-done.291) | copy-start | bytes 3076
  1867.8 174.2 %all-gather.23.cloned.1.call-start = ((), (), s32[]{:S(2)}) async-start(), calls=%async_computation.22 | async-start | bytes 9437184 | tf_op jit(solution)/shard_map/all_gather | solution.py:186
  1961.4 360.5 %reduce-scatter.23.cloned.1.call-start = ((), (), s32[]{:S(2)}) async-start(), calls=%async_computation.23 | async-start | bytes 9437184 | tf_op jit(solution)/shard_map/reduce_scatter | solution.py:204
  2197.6 561.0 %all-reduce.225.cloned.1.call-start = ((), (), s32[]{:S(2)}) async-start(), calls=%async_computation.24 | async-start | bytes 51380224 | tf_op jit(solution)/shard_map/psum | solution.py:216
  (308 other events, 2605.0 us)
Sparse Core Ops, SparseCore 0:
  13.4 84.7 all-gather.8
  236.7 87.9 reduce-scatter.8
  328.2 80.3 all-gather.10
  440.8 88.1 reduce-scatter.10
  534.4 80.4 all-gather.12
  783.9 87.9 reduce-scatter.12
  876.9 80.4 all-gather.14
  959.5 80.5 all-gather.16
  1078.0 88.1 reduce-scatter.16
  1171.6 80.3 all-gather.18
  1567.9 87.9 reduce-scatter.18
  1658.0 87.9 reduce-scatter.14
  1751.2 80.3 all-gather.20
  1867.9 88.1 reduce-scatter.20
  1961.6 80.3 all-gather.22
  2197.7 87.9 reduce-scatter.22
  2304.5 453.9 all-reduce.224
where the time goes:
time: 2810 us; the launch traced here: 2790 us
  waiting for transfers between devices  1600 us (57%)
  local copies, waits for them, and re-layouts  506 us (18%)
  matrix products  291 us (10%)
  other arithmetic  255 us (9%)
  blocking collectives  116 us (4%)
    psum x1, waiting for transfers between devices, local(): lax.psum(jnp.stack(mix_grads).astype(jnp.bfloat16), 'dp')  391 us
    all_gather x4, waiting for transfers between devices, local(): lax.all_gather(grad_stream.astype(jnp.bfloat16), 'mp', axis=0, tiled=True)  305 us
    pad x176, local copies, waits for them, and re-layouts, recurrence(): lax.associative_scan(combine, (forget.reshape(seq_shape), update.reshape(...  261 us
    slice x174, local copies, waits for them, and re-layouts, recurrence(): lax.associative_scan(combine, (forget.reshape(seq_shape), update.reshape(...  183 us
    reduce_scatter x2, waiting for transfers between devices, local(): lax.psum_scatter(glu_back_rows(jnp.int32(0), local_rows * lax.axis_size('...  176 us
    reduce_scatter x2, waiting for transfers between devices, local(): lax.psum_scatter(down_rows(jnp.int32(0), local_rows * lax.axis_size('mp')...  176 us
    reduce_scatter x2, waiting for transfers between devices, local(): lax.psum_scatter(out_rows(jnp.int32(0), local_rows * lax.axis_size('mp'))...  175 us
    all_gather x2, waiting for transfers between devices, local(): lax.all_gather(glu_normed.astype(jnp.bfloat16), 'mp', axis=0, tiled=True)  157 us
  transfers between devices with their start and end apart: 17, of which 16 were waited for; matrix products, arithmetic and copies ran while one was open for 6% of the time, Pallas kernels for 0%

commit v1 on v0

v1 whole, which is shorter than its diff:
```python
import functools

import jax
import jax.numpy as jnp
from jax import lax
from jax.experimental import pallas as pl
from jax.experimental.pallas import tpu as pltpu
from jax.sharding import PartitionSpec as P

norm_eps = 1e-06
domain_scale = (1.0, 0.5, 2.0)
F32 = jnp.float32
BF16 = jnp.bfloat16
LANES = 128
VMEM_LIMIT = 56 * 1024 * 1024


def high_bit(s):
    return 1 << (s.bit_length() - 1)


def low_bit(s):
    return s & -s


def swap_dp(v, bit):
    return lax.ppermute(v, "dp", [(i, i ^ bit) for i in range(lax.axis_size("dp"))])


def swap_core(v):
    return lax.ppermute(v, "mp", [(i, i ^ 1) for i in range(lax.axis_size("mp"))])


def plane_gather(x):
    count = lax.axis_size("dp")
    half = x.shape[0] // 2
    first = {0: x[:half]}
    last = {0: x[half:]}
    for s in range(1, count):
        first[s] = swap_dp(first[s ^ high_bit(s)], high_bit(s))
        last[s] = swap_dp(last[s ^ low_bit(s)], low_bit(s))
    slots = []
    for s in range(count):
        own = x if s == 0 else jnp.concatenate([first[s], last[s]], 0)
        slots.append(jnp.concatenate([own, swap_core(own)], 0))
    return slots


def bit_flip(s, bits):
    return int(format(s, "0" + str(bits) + "b")[::-1], 2)


def plane_scatter(parts):
    count = len(parts)
    bits = max(count.bit_length() - 1, 1)
    rows = parts[0].shape[0] // 2
    half = rows // 2
    first = {}
    last = {}
    for s in reversed(range(count)):
        both = parts[s][:rows].astype(F32) + swap_core(parts[s][rows:]).astype(F32)
        first[s] = both[:half]
        last[s] = both[half:]
    for s in reversed(range(1, count)):
        bit = high_bit(s)
        first[s ^ bit] = first[s ^ bit] + swap_dp(first[s].astype(BF16), bit).astype(F32)
    for s in sorted(range(1, count), key=lambda s: -bit_flip(s, bits)):
        bit = low_bit(s)
        last[s ^ bit] = last[s ^ bit] + swap_dp(last[s].astype(BF16), bit).astype(F32)
    return jnp.concatenate([first[0], last[0]], 0)


def plane_scatter_rows(totals):
    part = totals[:, 0] + swap_core(totals[:, 1])
    while part.shape[0] > 1:
        half = part.shape[0] // 2
        part = part[:half] + swap_dp(part[half:], half)
    return part[0]


def plane_gather_rows(vec):
    part = jnp.stack([vec, swap_core(vec)], 0)[None]
    while part.shape[0] < lax.axis_size("dp"):
        part = jnp.concatenate([part, swap_dp(part, part.shape[0])], 0)
    return part.reshape(-1, vec.shape[0])


def line_groups():
    size = lax.axis_size("mp")
    return [[place * 2 + core for place in range(size // 2)] for core in (0, 1)]


def line_gather(v):
    return lax.all_gather(v, "mp", axis=0, tiled=False, axis_index_groups=line_groups())


def line_scatter(v):
    return lax.psum_scatter(
        v, "mp", scatter_dimension=0, tiled=False, axis_index_groups=line_groups()
    )


def line_carry(decay, value, ahead):
    size = lax.axis_size("mp")
    packed = jnp.stack([decay, value], 0)
    total = None
    for step in reversed(range(1, size // 2)):
        pairs = [(i, i + 2 * step) for i in range(size - 2 * step)]
        if ahead:
            pairs = [(b, a) for a, b in pairs]
        got = lax.ppermute(packed, "mp", pairs)
        total = got[1] if total is None else got[1] + got[0] * total
    return jnp.zeros_like(value) if total is None else total


def in_order(core, own, other):
    return jnp.where(core == 0, own, other), jnp.where(core == 0, other, own)


def scan_kernel(slots, core_ref, *refs):
    inputs, forgets, rest = refs[:slots], refs[slots : 2 * slots], refs[2 * slots :]
    bound_ref, local_ref, decay_ref, end_ref, full_ref, seq_end_ref, seq_full_ref = rest
    pair = inputs[0].shape[0]
    rows = pair // 2
    blocks = 2 * slots
    low = bound_ref[...]
    for s in range(slots):
        forget = low + (1.0 - low) * jax.nn.sigmoid(forgets[s][...])
        decay_ref[pl.ds(s * pair, pair), :] = forget
        local_ref[pl.ds(s * pair, pair), :] = (1.0 - forget) * jax.nn.silu(inputs[s][...])

    def step(t, kept):
        state, decay = kept
        place = pl.ds(t, blocks, stride=rows)
        forget = decay_ref[place, :]
        state = forget * state + local_ref[place, :]
        decay = forget * decay
        local_ref[place, :] = state
        decay_ref[place, :] = decay
        return state, decay

    none = decay_ref[pl.ds(0, blocks, stride=rows), :] * 0.0
    end, full = lax.fori_loop(0, rows, step, (none, none + 1.0), unroll=8)
    end_ref[...] = end
    full_ref[...] = full
    core = core_ref[0]
    own, other = pl.ds(0, slots, stride=2), pl.ds(1, slots, stride=2)
    end_a, end_b = in_order(core, end_ref[own, :], end_ref[other, :])
    full_a, full_b = in_order(core, full_ref[own, :], full_ref[other, :])
    seq_end_ref[...] = end_b + full_b * end_a
    seq_full_ref[...] = full_a * full_b


def state_kernel(slots, core_ref, *refs):
    gates, rest = refs[:slots], refs[slots:]
    local_ref, decay_ref, end_ref, full_ref, enter_ref, gain_ref = rest[:6]
    state_ref, square_ref, carry_ref = rest[6:9]
    outs = rest[9:]
    pair = gates[0].shape[0]
    rows = pair // 2
    core = core_ref[0]
    own, other = pl.ds(0, slots, stride=2), pl.ds(1, slots, stride=2)
    end_a, _ = in_order(core, end_ref[own, :], end_ref[other, :])
    full_a, _ = in_order(core, full_ref[own, :], full_ref[other, :])
    carry_a = enter_ref[...]
    carry_b = end_a + full_a * carry_a
    carry_own, carry_other = in_order(core, carry_a, carry_b)
    carry_ref[own, :] = carry_own
    carry_ref[other, :] = carry_other
    gain = gain_ref[...]
    for s in range(slots):
        for side in (0, 1):
            block = 2 * s + side
            here = pl.ds(block * rows, rows)
            state = local_ref[here, :] + decay_ref[here, :] * carry_ref[block : block + 1, :]
            state_ref[here, :] = state
            gated = state * jax.nn.silu(gates[s][pl.ds(side * rows, rows), :])
            outs[s][pl.ds(side * rows, rows), :] = (gated * gain).astype(BF16)
            total = jnp.sum((gated * gated).T, 0, keepdims=True)

            @pl.when(pl.program_id(0) == 0)
            def _(block=block, total=total):
                square_ref[block : block + 1, :] = total

            @pl.when(pl.program_id(0) > 0)
            def _(block=block, total=total):
                square_ref[block : block + 1, :] = square_ref[block : block + 1, :] + total


def across(row, lanes):
    return jnp.broadcast_to(row, (lanes, row.shape[1])).T


def scan_back_kernel(slots, core_ref, *refs):
    grads, forgets, gates, rest = (
        refs[:slots],
        refs[slots : 2 * slots],
        refs[2 * slots : 3 * slots],
        refs[3 * slots :],
    )
    state_ref, stat_ref, bound_ref, gain_ref = rest[:4]
    local_ref, decay_ref, end_ref, full_ref, seq_end_ref, seq_full_ref = rest[4:10]
    (forget_ref,) = rest[10:]
    pair = grads[0].shape[0]
    rows = pair // 2
    blocks = 2 * slots
    low = bound_ref[...]
    gain = gain_ref[...]
    for s in range(slots):
        for side in (0, 1):
            block = 2 * s + side
            here, part = pl.ds(block * rows, rows), pl.ds(side * rows, rows)
            silu_gate = jax.nn.silu(gates[s][part, :])
            gated = state_ref[here, :] * silu_gate
            dgated = grads[s][part, :] * gain - gated * across(
                stat_ref[block : block + 1, :], LANES
            )
            local_ref[here, :] = dgated * silu_gate
            forget_ref[here, :] = low + (1.0 - low) * jax.nn.sigmoid(forgets[s][part, :])

    def step(k, kept):
        t = rows - 1 - k
        state, decay, forget = kept
        place = pl.ds(t, blocks, stride=rows)
        state = forget * state + local_ref[place, :]
        decay = forget * decay
        local_ref[place, :] = state
        decay_ref[place, :] = decay
        return state, decay, forget_ref[place, :]

    none = forget_ref[pl.ds(0, blocks, stride=rows), :] * 0.0
    state, decay, forget = lax.fori_loop(
        0, rows, step, (none, none + 1.0, none + 1.0), unroll=8
    )
    end_ref[...] = forget * state
    full_ref[...] = forget * decay
    core = core_ref[0]
    own, other = pl.ds(0, slots, stride=2), pl.ds(1, slots, stride=2)
    end_a, end_b = in_order(core, end_ref[own, :], end_ref[other, :])
    full_a, full_b = in_order(core, full_ref[own, :], full_ref[other, :])
    seq_end_ref[...] = end_a + full_a * end_b
    seq_full_ref[...] = full_a * full_b


def project_back_kernel(slots, core_ref, *refs):
    grads, inputs, forgets, gates, rest = (
        refs[:slots],
        refs[slots : 2 * slots],
        refs[2 * slots : 3 * slots],
        refs[3 * slots : 4 * slots],
        refs[4 * slots :],
    )
    state_ref, stat_ref, bound_ref, gain_ref, carry_ref = rest[:5]
    local_ref, decay_ref, end_ref, full_ref, enter_ref = rest[5:10]
    out_ref, bound_grad_ref, gain_grad_ref, back_ref = rest[10:]
    pair = grads[0].shape[0]
    rows = pair // 2
    core = core_ref[0]
    width = out_ref.shape[1] // 3
    column = pl.program_id(0) * LANES
    own, other = pl.ds(0, slots, stride=2), pl.ds(1, slots, stride=2)
    _, end_b = in_order(core, end_ref[own, :], end_ref[other, :])
    _, full_b = in_order(core, full_ref[own, :], full_ref[other, :])
    carry_b = enter_ref[...]
    carry_a = end_b + full_b * carry_b
    carry_own, carry_other = in_order(core, carry_a, carry_b)
    back_ref[own, :] = carry_own
    back_ref[other, :] = carry_other
    low = bound_ref[...]
    gain = gain_ref[...]
    bound_total = jnp.zeros((1, LANES), F32)
    gain_total = jnp.zeros((1, LANES), F32)
    top = lax.broadcasted_iota(jnp.int32, (rows, LANES), 0) == 0
    for s in range(slots):
        for side in (0, 1):
            block = 2 * s + side
            here, part = pl.ds(block * rows, rows), pl.ds(side * rows, rows)
            state = state_ref[here, :]
            before = jnp.where(top, carry_ref[block : block + 1, :], pltpu.roll(state, 1, 0))
            gate = gates[s][part, :]
            gate_sig = jax.nn.sigmoid(gate)
            silu_gate = gate * gate_sig
            grad = grads[s][part, :]
            gated = state * silu_gate
            dgated = grad * gain - gated * across(stat_ref[block : block + 1, :], LANES)
            dstate = local_ref[here, :] + decay_ref[here, :] * back_ref[block : block + 1, :]
            enter = inputs[s][part, :]
            enter_sig = jax.nn.sigmoid(enter)
            forget_sig = jax.nn.sigmoid(forgets[s][part, :])
            keep = (1.0 - low) * (1.0 - forget_sig)
            dforget = dstate * (before - enter * enter_sig)
            slope = dforget * (1.0 - forget_sig)
            dinput = dstate * keep * enter_sig * (1.0 + enter * (1.0 - enter_sig))
            dpre = slope * (1.0 - low) * forget_sig
            dgate = dgated * state * gate_sig * (1.0 + gate * (1.0 - gate_sig))
            out_ref[here, pl.ds(pl.multiple_of(column, LANES), LANES)] = dinput.astype(BF16)
            out_ref[here, pl.ds(pl.multiple_of(width + column, LANES), LANES)] = dpre.astype(BF16)
            out_ref[here, pl.ds(pl.multiple_of(2 * width + column, LANES), LANES)] = dgate.astype(
                BF16
            )
            bound_total = bound_total + jnp.sum(slope, 0, keepdims=True)
            gain_total = gain_total + jnp.sum(grad * gated, 0, keepdims=True)
    bound_grad_ref[...] = bound_total
    gain_grad_ref[...] = gain_total


def column_block(rows, offset=0):
    return pl.BlockSpec((rows, LANES), lambda i, offset=offset: (0, offset + i))


def kernel_call(body, name, steps, in_specs, out_specs, out_shapes, scratch, flops, args):
    moved = sum(a.size * a.dtype.itemsize for a in args)
    moved += sum(s.size * s.dtype.itemsize for s in out_shapes)
    return pl.pallas_call(
        body,
        name=name,
        grid=(steps,),
        in_specs=[pl.BlockSpec(memory_space=pltpu.SMEM)] + in_specs,
        out_specs=out_specs,
        out_shape=out_shapes,
        scratch_shapes=scratch,
        compiler_params=pltpu.CompilerParams(
            vmem_limit_bytes=VMEM_LIMIT, dimension_semantics=("arbitrary",)
        ),
        cost_estimate=pl.CostEstimate(flops=flops, bytes_accessed=moved, transcendentals=0),
    )(*args)


def struct(shape, dtype=F32):
    return jax.ShapeDtypeStruct(shape, dtype)


def mixer_scan(core, projected, bound):
    slots = len(projected)
    pair = projected[0].shape[0]
    channels = projected[0].shape[1] // 3
    steps = channels // LANES
    total = pair * slots
    return kernel_call(
        functools.partial(scan_kernel, slots),
        "mixer_scan",
        steps,
        [column_block(pair)] * slots + [column_block(pair, steps)] * slots + [column_block(1)],
        [column_block(total)] * 2 + [column_block(2 * slots)] * 2 + [column_block(slots)] * 2,
        [struct((total, channels))] * 2
        + [struct((2 * slots, channels))] * 2
        + [struct((slots, channels))] * 2,
        [],
        total * channels * 200,
        [core] + projected + projected + [bound],
    )


def mixer_state(core, projected, local, decay, end, full, enter, gain):
    slots = len(projected)
    pair = projected[0].shape[0]
    channels = projected[0].shape[1] // 3
    steps = channels // LANES
    total = pair * slots
    outs = kernel_call(
        functools.partial(state_kernel, slots),
        "mixer_state",
        steps,
        [column_block(pair, 2 * steps)] * slots
        + [column_block(total)] * 2
        + [column_block(2 * slots)] * 2
        + [column_block(slots), column_block(1)],
        [
            column_block(total),
            pl.BlockSpec((2 * slots, pair // 2), lambda i: (0, 0)),
            column_block(2 * slots),
        ]
        + [column_block(pair)] * slots,
        [
            struct((total, channels)),
            struct((2 * slots, pair // 2)),
            struct((2 * slots, channels)),
        ]
        + [struct((pair, channels), BF16)] * slots,
        [],
        total * channels * 100,
        [core] + projected + [local, decay, end, full, enter, gain],
    )
    return outs[0], outs[1], outs[2], list(outs[3:])


def mixer_scan_back(core, grads, projected, state, stat, bound, gain):
    slots = len(projected)
    pair = projected[0].shape[0]
    channels = projected[0].shape[1] // 3
    steps = channels // LANES
    total = pair * slots
    return kernel_call(
        functools.partial(scan_back_kernel, slots),
        "mixer_scan_back",
        steps,
        [column_block(pair)] * slots
        + [column_block(pair, steps)] * slots
        + [column_block(pair, 2 * steps)] * slots
        + [column_block(total)]
        + [pl.BlockSpec((2 * slots, pair // 2), lambda i: (0, 0))]
        + [column_block(1)] * 2,
        [column_block(total)] * 2 + [column_block(2 * slots)] * 2 + [column_block(slots)] * 2,
        [struct((total, channels))] * 2
        + [struct((2 * slots, channels))] * 2
        + [struct((slots, channels))] * 2,
        [pltpu.VMEM((total, LANES), F32)],
        total * channels * 200,
        [core] + grads + projected + projected + [state, stat, bound, gain],
    )


def mixer_project_back(
    core, grads, projected, state, stat, bound, gain, carry, local, decay, end, full, enter
):
    slots = len(projected)
    pair = projected[0].shape[0]
    channels = projected[0].shape[1] // 3
    steps = channels // LANES
    total = pair * slots
    return kernel_call(
        functools.partial(project_back_kernel, slots),
        "mixer_project_back",
        steps,
        [column_block(pair)] * slots
        + [column_block(pair)] * slots
        + [column_block(pair, steps)] * slots
        + [column_block(pair, 2 * steps)] * slots
        + [column_block(total)]
        + [pl.BlockSpec((2 * slots, pair // 2), lambda i: (0, 0))]
        + [column_block(1)] * 2
        + [column_block(2 * slots)]
        + [column_block(total)] * 2
        + [column_block(2 * slots)] * 2
        + [column_block(slots)],
        [pl.BlockSpec((total, 3 * channels), lambda i: (0, 0))] + [column_block(1)] * 2,
        [struct((total, 3 * channels), BF16)] + [struct((1, channels))] * 2,
        [pltpu.VMEM((2 * slots, LANES), F32)],
        total * channels * 200,
        [core]
        + grads
        + projected * 3
        + [state, stat, bound, gain, carry, local, decay, end, full, enter],
    )


def matmul(a, b):
    return jnp.dot(a, b, preferred_element_type=F32)


def matmul_t(a, b):
    return lax.dot_general(a, b, (((1,), (1,)), ((), ())), preferred_element_type=F32)


def matmul_rows(a, b):
    return lax.dot_general(a, b, (((0,), (0,)), ((), ())), preferred_element_type=F32)


def rms_factor(values):
    return lax.rsqrt(jnp.mean(values * values, -1, keepdims=True) + norm_eps)


def rms_back(values, gain, grad):
    factor = rms_factor(values)
    normed = values * factor
    scaled = grad * gain
    back = factor * (scaled - normed * jnp.mean(scaled * normed, -1, keepdims=True))
    return back, jnp.sum(grad * normed, 0)


def bound_rows(logits):
    return jnp.cumsum(jax.nn.softmax(logits, 0), 0)


def local(
    hidden_in,
    cotangent,
    domain_tags,
    mix_weight,
    mix_out_weight,
    glu_weight,
    glu_out_weight,
    mix_gain,
    out_gain,
    glu_gain,
    bound_logits,
):
    dp = lax.axis_size("dp")
    line = lax.axis_size("mp") // 2
    column = lax.axis_index("dp")
    member = lax.axis_index("mp")
    core = member % 2
    core_arg = core.astype(jnp.int32).reshape(1)
    width = hidden_in.shape[1]
    layers = mix_weight.shape[0]
    channels = mix_weight.shape[3]
    units = glu_weight.shape[3]
    c_strip, u_strip = channels // dp, units // dp

    def cut(array, axis, size):
        return lax.dynamic_slice_in_dim(array, column * size, size, axis)

    mix_w, out_w, gate_w, up_w, down_w = [], [], [], [], []
    for l in range(layers):
        mix_strip = cut(mix_weight[l], 2, c_strip).transpose(1, 2, 0).reshape(3 * c_strip, width)
        out_strip = cut(mix_out_weight[l], 0, c_strip)
        glu_strip = cut(glu_weight[l], 2, u_strip).transpose(1, 2, 0).reshape(2 * u_strip, width)
        down_strip = cut(glu_out_weight[l], 0, u_strip)
        got = line_gather(mix_strip).reshape(line, 3, c_strip, width)
        mix_w.append(got.transpose(1, 0, 2, 3).reshape(3 * line * c_strip, width))
        got = line_gather(jnp.concatenate([out_strip, glu_strip, down_strip], 0))
        out_w.append(got[:, :c_strip].reshape(line * c_strip, width))
        start = c_strip
        gate_w.append(got[:, start : start + u_strip].reshape(line * u_strip, width))
        start += u_strip
        up_w.append(got[:, start : start + u_strip].reshape(line * u_strip, width))
        start += u_strip
        down_w.append(got[:, start : start + u_strip].reshape(line * u_strip, width))
    bound_vals, bound_back = jax.vjp(bound_rows, bound_logits)
    small = jnp.concatenate([cut(bound_vals, 1, c_strip), cut(out_gain, 1, c_strip)], 0)
    small = line_gather(small).transpose(1, 0, 2).reshape(-1, line * c_strip)
    bounds = [small[l : l + 1] for l in range(layers)]
    gains = [small[bound_vals.shape[0] + l :][:1] for l in range(layers)]

    stream = hidden_in.astype(F32)
    kept = []
    for l in range(layers):
        stream_in = stream
        mixer_in = plane_gather((stream * rms_factor(stream) * mix_gain[l]).astype(BF16))
        projected = [matmul_t(rows, mix_w[l]) for rows in mixer_in]
        scanned, decay, end, full, seq_end, seq_full = mixer_scan(core_arg, projected, bounds[l])
        enter = line_carry(seq_full, seq_end, False)
        state, squares, carry, mixed = mixer_state(
            core_arg, projected, scanned, decay, end, full, enter, gains[l]
        )
        parts = [matmul(rows, out_w[l]).astype(BF16) for rows in mixed]
        total = plane_scatter_rows(squares.reshape(dp, 2, -1))
        out_factor = lax.rsqrt(total / width + norm_eps)[:, None]
        raw = plane_scatter(parts)
        stream_mid = stream + raw * out_factor
        glu_in = plane_gather((stream_mid * rms_factor(stream_mid) * glu_gain[l]).astype(BF16))
        gate = [matmul_t(rows, gate_w[l]) for rows in glu_in]
        up = [matmul_t(rows, up_w[l]) for rows in glu_in]
        hidden = [(jax.nn.silu(a) * b).astype(BF16) for a, b in zip(gate, up)]
        parts = [matmul(rows, down_w[l]).astype(BF16) for rows in hidden]
        stream = stream_mid + plane_scatter(parts)
        kept.append(
            (
                stream_in,
                mixer_in,
                projected,
                state,
                carry,
                mixed,
                out_factor,
                raw,
                stream_mid,
                glu_in,
                gate,
                up,
                hidden,
            )
        )

    scale_table = jnp.array(domain_scale, dtype=F32)
    match = domain_tags[0] == jnp.arange(3, dtype=jnp.int32)
    grad = cotangent.astype(F32) * jnp.sum(jnp.where(match, scale_table, 0.0))
    mix_grads = [None] * layers
    mix_out_grads = [None] * layers
    glu_grads = [None] * layers
    glu_out_grads = [None] * layers
    mix_gain_parts = [None] * layers
    glu_gain_parts = [None] * layers
    out_gain_parts = [None] * layers
    bound_parts = [None] * layers
    for l in reversed(range(layers)):
        (
            stream_in,
            mixer_in,
            projected,
            state,
            carry,
            mixed,
            out_factor,
            raw,
            stream_mid,
            glu_in,
            gate,
            up,
            hidden,
        ) = kept[l]
        down_grad = plane_gather(grad.astype(BF16))
        parts, dgates, dups = [], [], []
        for s in range(dp):
            dhidden = matmul_t(down_grad[s], down_w[l])
            sig = jax.nn.sigmoid(gate[s])
            dgates.append((dhidden * up[s] * sig * (1.0 + gate[s] * (1.0 - sig))).astype(BF16))
            dups.append((dhidden * gate[s] * sig).astype(BF16))
            parts.append((matmul(dgates[s], gate_w[l]) + matmul(dups[s], up_w[l])).astype(BF16))
        back, glu_gain_parts[l] = rms_back(stream_mid, glu_gain[l], plane_scatter(parts))
        glu_rows = jnp.concatenate(glu_in, 0)
        down_part = matmul_rows(jnp.concatenate(hidden, 0), jnp.concatenate(down_grad, 0))
        gate_part = matmul_rows(jnp.concatenate(dgates, 0), glu_rows)
        up_part = matmul_rows(jnp.concatenate(dups, 0), glu_rows)
        sent = jnp.concatenate(
            [v.astype(BF16).reshape(line, u_strip, width) for v in (down_part, gate_part, up_part)],
            1,
        )
        strips = lax.all_gather(line_scatter(sent), "dp", axis=0)
        glu_out_grads[l] = strips[:, :u_strip].reshape(units, width).astype(F32)
        glu_grads[l] = (
            strips[:, u_strip:]
            .reshape(dp, 2, u_strip, width)
            .transpose(3, 1, 0, 2)
            .reshape(width, 2, units)
            .astype(F32)
        )
        grad = grad + back

        out_low = (grad * out_factor).astype(BF16)
        stat = jnp.mean(out_low.astype(F32) * raw, -1) * (out_factor * out_factor)[:, 0]
        stats = plane_gather_rows(stat)
        out_grad = plane_gather(out_low)
        mixed_grad = [matmul_t(rows, out_w[l]) for rows in out_grad]
        scanned, decay, end, full, seq_end, seq_full = mixer_scan_back(
            core_arg, mixed_grad, projected, state, stats, bounds[l], gains[l]
        )
        enter = line_carry(seq_full, seq_end, True)
        proj_grad, bound_parts[l], out_gain_parts[l] = mixer_project_back(
            core_arg,
            mixed_grad,
            projected,
            state,
            stats,
            bounds[l],
            gains[l],
            carry,
            scanned,
            decay,
            end,
            full,
            enter,
        )
        pair = projected[0].shape[0]
        parts = [
            matmul(proj_grad[s * pair : (s + 1) * pair], mix_w[l]).astype(BF16) for s in range(dp)
        ]
        mix_part = matmul_rows(proj_grad, jnp.concatenate(mixer_in, 0))
        out_part = matmul_rows(jnp.concatenate(mixed, 0), jnp.concatenate(out_grad, 0))
        mix_sent = mix_part.astype(BF16).reshape(3, line, c_strip, width).transpose(1, 0, 2, 3)
        sent = jnp.concatenate(
            [
                mix_sent.reshape(line, 3 * c_strip, width),
                out_part.astype(BF16).reshape(line, c_strip, width),
            ],
            1,
        )
        strips = lax.all_gather(line_scatter(sent), "dp", axis=0)
        mix_out_grads[l] = strips[:, 3 * c_strip :].reshape(channels, width).astype(F32)
        mix_grads[l] = (
            strips[:, : 3 * c_strip]
            .reshape(dp, 3, c_strip, width)
            .transpose(3, 1, 0, 2)
            .reshape(width, 3, channels)
            .astype(F32)
        )
        back, mix_gain_parts[l] = rms_back(stream_in, mix_gain[l], plane_scatter(parts))
        grad = grad + back

    def spread(row):
        zeros = jnp.zeros((line, 2, dp, c_strip), F32)
        return lax.dynamic_update_slice(
            zeros, row.reshape(line, 1, 1, c_strip), (0, core, column, 0)
        ).reshape(-1)

    rows = jnp.stack(
        mix_gain_parts
        + glu_gain_parts
        + [spread(v) for v in out_gain_parts]
        + [spread(v) for v in bound_parts]
    )
    rows = lax.psum(rows, ("dp", "mp"))
    mix_gain_grad = rows[:layers]
    glu_gain_grad = rows[layers : 2 * layers]
    mine = lax.dynamic_slice_in_dim(rows[2 * layers :], member * channels, channels, 1)
    out_gain_grad = mine[:layers]
    extra = jnp.zeros((bound_vals.shape[0] - layers, channels), F32)
    bound_grad = bound_back(jnp.concatenate([mine[layers:], extra], 0))[0]
    return (
        stream,
        grad,
        jnp.stack(mix_grads),
        jnp.stack(mix_out_grads),
        jnp.stack(glu_grads),
        jnp.stack(glu_out_grads),
        mix_gain_grad,
        out_gain_grad,
        glu_gain_grad,
        bound_grad,
    )


def solution(mesh):
    return jax.shard_map(
        local,
        mesh=mesh,
        in_specs=(
            P(("dp", "mp"), None),
            P(("dp", "mp"), None),
            P("dp"),
            P(None, None, None, "mp"),
            P(None, "mp", None),
            P(None, None, None, "mp"),
            P(None, "mp", None),
            P(),
            P(None, "mp"),
            P(),
            P(None, "mp"),
        ),
        out_specs=(
            P(("dp", "mp"), None),
            P(("dp", "mp"), None),
            P(None, None, None, "mp"),
            P(None, "mp", None),
            P(None, None, None, "mp"),
            P(None, "mp", None),
            P(),
            P(None, "mp"),
            P(),
            P(None, "mp"),
        ),
        check_vma=False,
    )
```

time: 2810 us -> 2030 us (0.72)
  waiting for transfers between devices: 1600 us -> 1140 us
  local copies, waits for them, and re-layouts: 506 us -> 233 us
  starting transfers between devices: 1.58 us -> 158 us
  other arithmetic: 255 us -> 124 us
  blocking collectives: 116 us -> 13.8 us
  Pallas kernels: 0 us -> 71.3 us
    ppermute x0 -> x184, waiting for transfers between devices: none -> 370 us  [the longest x104 368 us: swap_dp(): lax.ppermute(v, 'dp', [(i, i ^ bit) for i in range(lax.axis_size('dp'))])]
    reduce_scatter x8 -> x4, waiting for transfers between devices: 603 us -> 242 us  [line_scatter(): lax.psum_scatter(v, 'mp', scatter_dimension=0, tiled=False, axis_index_gr...]
    psum x1, waiting for transfers between devices: 391 us -> 121 us  [local(): rows = lax.psum(rows, ('dp', 'mp'))]
    pad x176 -> x0, local copies, waits for them, and re-layouts: 261 us -> none  [recurrence(): lax.associative_scan(combine, (forget.reshape(seq_shape), update.reshape(...]
    all_gather x8, waiting for transfers between devices: 610 us -> 406 us  [the longest x4 257 us: local(): strips = lax.all_gather(line_scatter(sent), 'dp', axis=0)]
    ppermute x0 -> x184, starting transfers between devices: none -> 157 us  [the longest x104 117 us: swap_dp(): lax.ppermute(v, 'dp', [(i, i ^ bit) for i in range(lax.axis_size('dp'))])]
    slice x180 -> x104, local copies, waits for them, and re-layouts: 201 us -> 73.3 us  [the longest x1 11.7 us: local(): glu_weight[l]]
    psum x6 -> x0, blocking collectives: 116 us -> none  [the longest x1 38.3 us: local(): lax.psum((jnp.stack(mix_gain_parts), jnp.stack(glu_gain_parts)), ('dp', '...]
  transfers between devices with their start and end apart: 17 -> 197, of which waited for: 16 -> 59; matrix products, arithmetic and copies ran while one was open for 6% -> 27% of each run, Pallas kernels for 0% -> 2%
where the time goes in v1:
time: 2030 us; the launch traced here: 2020 us
  waiting for transfers between devices  1140 us (56%)
  matrix products  266 us (13%)
  local copies, waits for them, and re-layouts  233 us (11%)
  starting transfers between devices  158 us (8%)
  other arithmetic  124 us (6%)
  Pallas kernels  71.3 us (4%)
    ppermute x104, waiting for transfers between devices, swap_dp(): lax.ppermute(v, 'dp', [(i, i ^ bit) for i in range(lax.axis_size('dp'))])  368 us
    all_gather x4, waiting for transfers between devices, local(): strips = lax.all_gather(line_scatter(sent), 'dp', axis=0)  257 us
    reduce_scatter x4, waiting for transfers between devices, line_scatter(): lax.psum_scatter(v, 'mp', scatter_dimension=0, tiled=False, axis_index_gr...  242 us
    all_gather x4, waiting for transfers between devices, line_gather(): lax.all_gather(v, 'mp', axis=0, tiled=False, axis_index_groups=line_group...  149 us
    unnamed x495, local copies, waits for them, and re-layouts  122 us
    psum x1, waiting for transfers between devices, local(): rows = lax.psum(rows, ('dp', 'mp'))  121 us
    dot_general x40, matrix products, matmul_t(): lax.dot_general(a, b, (((1,), (1,)), ((), ())), preferred_element_type=F32)  119 us
    ppermute x104, starting transfers between devices, swap_dp(): lax.ppermute(v, 'dp', [(i, i ^ bit) for i in range(lax.axis_size('dp'))])  117 us
  transfers between devices with their start and end apart: 197, of which 59 were waited for; matrix products, arithmetic and copies ran while one was open for 27% of the time, Pallas kernels for 2%

profile of v1, /device:TPU:0, one launch (start us, length us, event | category | flops | bytes accessed | tf_op | source)
XLA Modules:
  0.0 2024.5 jit_solution(9428156919286208401)
XLA Ops:
  25.2 11.7 fusion.304
  67.3 13.8 all-gather.3
  167.2 90.0 %all-gather.25.cloned.1.call-done = bf16[2368,2048]{1,0:T(8,128)(2,1)} async-done(((bf16[592,2048]{1,0:T(8,128)(2,1)}), bf16[2368,2048]{1,0:T(8,128)(2,1)}) %all-gather.25.cloned.1.call-update) | async-done | bytes 9699344 | tf_op jit(solution)/shard_map/all_gather | solution.py:94
  268.8 9.7 collective-permute-done.18
  291.3 10.2 collective-permute-done.19
  378.5 12.3 collective-permute-done.44
  433.8 59.1 %all-gather.27.cloned.1.call-done = bf16[2368,2048]{1,0:T(8,128)(2,1)} async-done(((bf16[592,2048]{1,0:T(8,128)(2,1)}), bf16[2368,2048]{1,0:T(8,128)(2,1)}) %all-gather.27.cloned.1.call-update) | async-done | bytes 9699344 | tf_op jit(solution)/shard_map/all_gather | solution.py:94
  572.3 19.5 collective-permute-done.64
  594.6 10.5 collective-permute-done.65
  622.5 10.8 collective-permute-done.79
  726.3 18.4 collective-permute-done.87
  772.7 9.4 collective-permute-done.109
  805.8 19.1 collective-permute-done.124
  870.3 12.0 mixer_scan_back.2
  920.7 9.7 collective-permute-done.133
  942.4 10.5 collective-permute-done.134
  970.0 12.5 collective-permute-done.145
  1037.1 11.2 collective-permute-done.153
  1085.6 19.5 collective-permute-done.170
  1149.8 12.0 mixer_scan_back.3
  1174.0 9.5 mixer_project_back.3
  1183.5 10.2 convolution_convert_fusion.1
  1209.8 9.4 convolution_convert_fusion.2
  1324.6 10.5 collective-permute-done.180
  1338.5 89.6 %reduce-scatter.11.cloned.1.call-done = bf16[1,528,2048]{2,1,0:T(8,128)(2,1)} async-done(((bf16[4,528,2048]{2,1,0:T(8,128)(2,1)}), bf16[1,528,2048]{2,1,0:T(8,128)(2,1)}) %reduce-scatter.11.cloned.1.call-update) | async-done | bytes 2162704 | tf_op jit(solution)/shard_map/reduce_scatter | solution.py:98
  1428.4 152.1 %reduce-scatter.9.cloned.1.call-done = bf16[1,528,2048]{2,1,0:T(8,128)(2,1)} async-done(((bf16[4,528,2048]{2,1,0:T(8,128)(2,1)}), bf16[1,528,2048]{2,1,0:T(8,128)(2,1)}) %reduce-scatter.9.cloned.1.call-update) | async-done | bytes 2162704 | tf_op jit(solution)/shard_map/reduce_scatter | solution.py:98
  1584.0 121.0 %all-reduce.2.cloned.1.call-done = f32[8,2048]{1,0:T(8,128)} async-done(((f32[8,2048]{1,0:T(8,128)}), f32[8,2048]{1,0:T(8,128)}) %all-reduce.2.cloned.1.call-update) | async-done | bytes 65552 | tf_op jit(solution)/shard_map/psum | solution.py:682
  1708.6 51.6 %all-gather.19.cloned.1.call-done = bf16[4,256,2048]{2,1,0:T(8,128)(2,1)} async-done(((bf16[1,256,2048]{2,1,0:T(8,128)(2,1)}), bf16[4,256,2048]{2,1,0:T(8,128)(2,1)}) %all-gather.19.cloned.1.call-update) | async-done | bytes 4194320 | tf_op jit(solution)/shard_map/all_gather | solution.py:658
  1762.3 52.5 %all-gather.17.cloned.1.call-done = bf16[4,256,2048]{2,1,0:T(8,128)(2,1)} async-done(((bf16[1,256,2048]{2,1,0:T(8,128)(2,1)}), bf16[4,256,2048]{2,1,0:T(8,128)(2,1)}) %all-gather.17.cloned.1.call-update) | async-done | bytes 4194320 | tf_op jit(solution)/shard_map/all_gather | solution.py:658
  1822.7 13.1 copy.86
  1839.6 66.7 %all-gather.23.cloned.1.call-done = bf16[4,528,2048]{2,1,0:T(8,128)(2,1)} async-done(((bf16[1,528,2048]{2,1,0:T(8,128)(2,1)}), bf16[4,528,2048]{2,1,0:T(8,128)(2,1)}) %all-gather.23.cloned.1.call-update) | async-done | bytes 8650768 | tf_op jit(solution)/shard_map/all_gather | solution.py:609
  1912.0 86.0 %all-gather.21.cloned.1.call-done = bf16[4,528,2048]{2,1,0:T(8,128)(2,1)} async-done(((bf16[1,528,2048]{2,1,0:T(8,128)(2,1)}), bf16[4,528,2048]{2,1,0:T(8,128)(2,1)}) %all-gather.21.cloned.1.call-update) | async-done | bytes 8650768 | tf_op jit(solution)/shard_map/all_gather | solution.py:609
  (1284 shorter events, 951.5 us)
Async XLA Ops:
  7.2 104.9 %all-gather.13.cloned.1.call-start = ((), (), s32[]{:S(2)}) async-start(), calls=%async_computation.4 | async-start | bytes 3932160 | tf_op jit(solution)/shard_map/all_gather | solution.py:94
  18.7 238.4 %all-gather.25.cloned.1.call-start = ((), (), s32[]{:S(2)}) async-start(), calls=%async_computation.15 | async-start | bytes 12124160 | tf_op jit(solution)/shard_map/all_gather | solution.py:94
  41.9 383.9 %all-gather.15.cloned.1.call-start = ((), (), s32[]{:S(2)}) async-start(), calls=%async_computation.5 | async-start | bytes 3932160 | tf_op jit(solution)/shard_map/all_gather | solution.py:94
  44.8 448.1 %all-gather.27.cloned.1.call-start = ((), (), s32[]{:S(2)}) async-start(), calls=%async_computation.16 | async-start | bytes 12124160 | tf_op jit(solution)/shard_map/all_gather | solution.py:94
  63.7 1273.4 %reduce-scatter.7.cloned.1.call-start = ((), (), s32[]{:S(2)}) async-start(), calls=%async_computation.8 | async-start | bytes 5242880 | tf_op jit(solution)/shard_map/reduce_scatter | solution.py:98
  107.7 52.6 %collective-permute-start.103 = (bf16[128,2048]{1,0:T(8,128)(2,1)S(1)}, bf16[128,2048]{1,0:T(8,128)(2,1)S(1)}, u32[]{:S(2)}, u32[]{:S(2)}) collective-permute-start(bf16[128,2048]{1,0:T(8,128)(2,1)S(1)} %collective-permute-done.99), channel_id=1, source_target_pairs={{0,16},{8,24},{16,0},{24,8},{1,17},{9,25},{17,1},{25,9},{2,18},{10... | collective-permute-start | bytes 1572872 | tf_op jit(solution)/shard_map/ppermute | solution.py:27
  110.1 50.2 %collective-permute-start.104 = (bf16[128,2048]{1,0:T(8,128)(2,1)}, bf16[128,2048]{1,0:T(8,128)(2,1)}, u32[]{:S(2)}, u32[]{:S(2)}) collective-permute-start(bf16[128,2048]{1,0:T(8,128)(2,1)} %collective-permute-done.95), channel_id=1, source_target_pairs={{0,8},{8,0},{16,24},{24,16},{1,9},{9,1},{17,25},{25,17},{2,10},{10... | collective-permute-start | bytes 1572872 | tf_op jit(solution)/shard_map/ppermute | solution.py:27
  166.4 93.1 %collective-permute-start.25 = (f32[1,256]{1,0:T(1,128)S(1)}, f32[1,256]{1,0:T(1,128)S(1)}, u32[]{:S(2)}, u32[]{:S(2)}) collective-permute-start(f32[1,256]{1,0:T(1,128)S(1)} %slice.970), channel_id=1, source_target_pairs={{0,8},{8,0},{16,24},{24,16},{1,9},{9,1},{17,25},{25,17},{2,10},{10... | collective-permute-start | bytes 3080 | tf_op jit(solution)/shard_map/ppermute | solution.py:27
  348.3 52.7 %collective-permute-start.27 = (bf16[256,2048]{1,0:T(8,128)(2,1)S(1)}, bf16[256,2048]{1,0:T(8,128)(2,1)S(1)}, u32[]{:S(2)}, u32[]{:S(2)}) collective-permute-start(bf16[256,2048]{1,0:T(8,128)(2,1)S(1)} %slice.975), channel_id=1, source_target_pairs={{0,1},{1,0},{2,3},{3,2},{4,5},{5,4},{6,7},{7,6},{8,9},{9,8},{10,11... | collective-permute-start | bytes 3145736 | tf_op jit(solution)/shard_map/ppermute | solution.py:31
  429.8 71.0 %collective-permute-start.50 = (bf16[128,2048]{1,0:T(8,128)(2,1)}, bf16[128,2048]{1,0:T(8,128)(2,1)}, u32[]{:S(2)}, u32[]{:S(2)}) collective-permute-start(bf16[128,2048]{1,0:T(8,128)(2,1)} %get-tuple-element.250), channel_id=1, source_target_pairs={{0,16},{8,24},{16,0},{24,8},{1,17},{9,25},{17,1},{25,9},{2,18},{10... | collective-permute-start | bytes 1572872 | tf_op jit(solution)/shard_map/ppermute | solution.py:27
  430.4 71.8 %collective-permute-start.48 = (bf16[128,2048]{1,0:T(8,128)(2,1)}, bf16[128,2048]{1,0:T(8,128)(2,1)}, u32[]{:S(2)}, u32[]{:S(2)}) collective-permute-start(bf16[128,2048]{1,0:T(8,128)(2,1)} %get-tuple-element.251), channel_id=1, source_target_pairs={{0,8},{8,0},{16,24},{24,16},{1,9},{9,1},{17,25},{25,17},{2,10},{10... | collective-permute-start | bytes 1572872 | tf_op jit(solution)/shard_map/ppermute | solution.py:27
  430.9 74.8 %collective-permute-start.46 = (bf16[256,2048]{1,0:T(8,128)(2,1)}, bf16[256,2048]{1,0:T(8,128)(2,1)}, u32[]{:S(2)}, u32[]{:S(2)}) collective-permute-start(bf16[256,2048]{1,0:T(8,128)(2,1)} %get-tuple-element.155), channel_id=1, source_target_pairs={{0,1},{1,0},{2,3},{3,2},{4,5},{5,4},{6,7},{7,6},{8,9},{9,8},{10,11... | collective-permute-start | bytes 3145736 | tf_op jit(solution)/shard_map/ppermute | solution.py:31
  430.9 73.1 %collective-permute-start.53 = (bf16[128,2048]{1,0:T(8,128)(2,1)}, bf16[128,2048]{1,0:T(8,128)(2,1)}, u32[]{:S(2)}, u32[]{:S(2)}) collective-permute-start(bf16[128,2048]{1,0:T(8,128)(2,1)} %collective-permute-done.47), channel_id=1, source_target_pairs={{0,16},{8,24},{16,0},{24,8},{1,17},{9,25},{17,1},{25,9},{2,18},{10... | collective-permute-start | bytes 1572872 | tf_op jit(solution)/shard_map/ppermute | solution.py:27
  432.8 71.3 %collective-permute-start.54 = (bf16[128,2048]{1,0:T(8,128)(2,1)}, bf16[128,2048]{1,0:T(8,128)(2,1)S(1)}, u32[]{:S(2)}, u32[]{:S(2)}) collective-permute-start(bf16[128,2048]{1,0:T(8,128)(2,1)} %collective-permute-done.51), channel_id=1, source_target_pairs={{0,8},{8,0},{16,24},{24,16},{1,9},{9,1},{17,25},{25,17},{2,10},{10... | collective-permute-start | bytes 1572872 | tf_op jit(solution)/shard_map/ppermute | solution.py:27
  558.0 36.2 %collective-permute-start.59 = (bf16[256,2048]{1,0:T(8,128)(2,1)S(1)}, bf16[256,2048]{1,0:T(8,128)(2,1)S(1)}, u32[]{:S(2)}, u32[]{:S(2)}) collective-permute-start(bf16[256,2048]{1,0:T(8,128)(2,1)S(1)} %slice.1003), channel_id=1, source_target_pairs={{0,1},{1,0},{2,3},{3,2},{4,5},{5,4},{6,7},{7,6},{8,9},{9,8},{10,11... | collective-permute-start | bytes 3145736 | tf_op jit(solution)/shard_map/ppermute | solution.py:31
  633.3 44.9 %collective-permute-start.96 = (bf16[256,2048]{1,0:T(8,128)(2,1)S(1)}, bf16[256,2048]{1,0:T(8,128)(2,1)S(1)}, u32[]{:S(2)}, u32[]{:S(2)}) collective-permute-start(bf16[256,2048]{1,0:T(8,128)(2,1)S(1)} %copy-done.71), channel_id=1, source_target_pairs={{0,1},{1,0},{2,3},{3,2},{4,5},{5,4},{6,7},{7,6},{8,9},{9,8},{10,11... | collective-permute-start | bytes 3145736 | tf_op jit(solution)/shard_map/ppermute | solution.py:31
  655.2 45.5 %collective-permute-start.105 = (bf16[256,2048]{1,0:T(8,128)(2,1)S(1)}, bf16[256,2048]{1,0:T(8,128)(2,1)S(1)}, u32[]{:S(2)}, u32[]{:S(2)}) collective-permute-start(bf16[256,2048]{1,0:T(8,128)(2,1)S(1)} %copy-done.73), channel_id=1, source_target_pairs={{0,1},{1,0},{2,3},{3,2},{4,5},{5,4},{6,7},{7,6},{8,9},{9,8},{10,11... | collective-permute-start | bytes 3145736 | tf_op jit(solution)/shard_map/ppermute | solution.py:31
  657.7 38.1 %collective-permute-start.85 = (bf16[256,2048]{1,0:T(8,128)(2,1)}, bf16[256,2048]{1,0:T(8,128)(2,1)S(1)}, u32[]{:S(2)}, u32[]{:S(2)}) collective-permute-start(bf16[256,2048]{1,0:T(8,128)(2,1)} %pad_maximum_fusion.29), channel_id=1, source_target_pairs={{0,1},{1,0},{2,3},{3,2},{4,5},{5,4},{6,7},{7,6},{8,9},{9,8},{10,11... | collective-permute-start | bytes 3145736 | tf_op jit(solution)/shard_map/ppermute | solution.py:31
  665.6 46.1 %collective-permute-start.73 = (bf16[256,2048]{1,0:T(8,128)(2,1)}, bf16[256,2048]{1,0:T(8,128)(2,1)S(1)}, u32[]{:S(2)}, u32[]{:S(2)}) collective-permute-start(bf16[256,2048]{1,0:T(8,128)(2,1)} %slice.1028), channel_id=1, source_target_pairs={{0,1},{1,0},{2,3},{3,2},{4,5},{5,4},{6,7},{7,6},{8,9},{9,8},{10,11... | collective-permute-start | bytes 3145736 | tf_op jit(solution)/shard_map/ppermute | solution.py:31
  673.3 39.0 %collective-permute-start.93 = (bf16[256,2048]{1,0:T(8,128)(2,1)}, bf16[256,2048]{1,0:T(8,128)(2,1)}, u32[]{:S(2)}, u32[]{:S(2)}) collective-permute-start(bf16[256,2048]{1,0:T(8,128)(2,1)} %slice.1046), channel_id=1, source_target_pairs={{0,1},{1,0},{2,3},{3,2},{4,5},{5,4},{6,7},{7,6},{8,9},{9,8},{10,11... | collective-permute-start | bytes 3145736 | tf_op jit(solution)/shard_map/ppermute | solution.py:31
  678.2 35.9 %collective-permute-start.82 = (bf16[256,2048]{1,0:T(8,128)(2,1)S(1)}, bf16[256,2048]{1,0:T(8,128)(2,1)}, u32[]{:S(2)}, u32[]{:S(2)}) collective-permute-start(bf16[256,2048]{1,0:T(8,128)(2,1)S(1)} %slice.1036), channel_id=1, source_target_pairs={{0,1},{1,0},{2,3},{3,2},{4,5},{5,4},{6,7},{7,6},{8,9},{9,8},{10,11... | collective-permute-start | bytes 3145736 | tf_op jit(solution)/shard_map/ppermute | solution.py:31
  716.1 44.8 %collective-permute-start.89 = (bf16[128,2048]{1,0:T(8,128)(2,1)S(1)}, bf16[128,2048]{1,0:T(8,128)(2,1)S(1)}, u32[]{:S(2)}, u32[]{:S(2)}) collective-permute-start(bf16[128,2048]{1,0:T(8,128)(2,1)S(1)} %slice.1374), channel_id=1, source_target_pairs={{0,8},{8,0},{16,24},{24,16},{1,9},{9,1},{17,25},{25,17},{2,10},{10... | collective-permute-start | bytes 1572872 | tf_op jit(solution)/shard_map/ppermute | solution.py:27
  718.6 43.6 %collective-permute-start.78 = (bf16[128,2048]{1,0:T(8,128)(2,1)S(1)}, bf16[128,2048]{1,0:T(8,128)(2,1)S(1)}, u32[]{:S(2)}, u32[]{:S(2)}) collective-permute-start(bf16[128,2048]{1,0:T(8,128)(2,1)S(1)} %slice.1375), channel_id=1, source_target_pairs={{0,16},{8,24},{16,0},{24,8},{1,17},{9,25},{17,1},{25,9},{2,18},{10... | collective-permute-start | bytes 1572872 | tf_op jit(solution)/shard_map/ppermute | solution.py:27
  987.1 350.6 %reduce-scatter.5.cloned.1.call-start = ((), (), s32[]{:S(2)}) async-start(), calls=%async_computation.6 | async-start | bytes 5242880 | tf_op jit(solution)/shard_map/reduce_scatter | solution.py:98
  1005.3 53.7 %collective-permute-start.139 = (bf16[256,2048]{1,0:T(8,128)(2,1)S(1)}, bf16[256,2048]{1,0:T(8,128)(2,1)S(1)}, u32[]{:S(2)}, u32[]{:S(2)}) collective-permute-start(bf16[256,2048]{1,0:T(8,128)(2,1)S(1)} %slice.1087), channel_id=1, source_target_pairs={{0,1},{1,0},{2,3},{3,2},{4,5},{5,4},{6,7},{7,6},{8,9},{9,8},{10,11... | collective-permute-start | bytes 3145736 | tf_op jit(solution)/shard_map/ppermute | solution.py:31
  1196.6 231.4 %reduce-scatter.11.cloned.1.call-start = ((), (), s32[]{:S(2)}) async-start(), calls=%async_computation.12 | async-start | bytes 10813440 | tf_op jit(solution)/shard_map/reduce_scatter | solution.py:98
  1235.7 344.7 %reduce-scatter.9.cloned.1.call-start = ((), (), s32[]{:S(2)}) async-start(), calls=%async_computation.10 | async-start | bytes 10813440 | tf_op jit(solution)/shard_map/reduce_scatter | solution.py:98
  1274.5 430.5 %all-reduce.2.cloned.1.call-start = ((), (), s32[]{:S(2)}) async-start(), calls=%async_computation.14 | async-start | bytes 131072 | tf_op jit(solution)/shard_map/psum | solution.py:682
  1337.1 423.1 %all-gather.19.cloned.1.call-start = ((), (), s32[]{:S(2)}) async-start(), calls=%async_computation.9 | async-start | bytes 5242880 | tf_op jit(solution)/shard_map/all_gather | solution.py:658
  1337.7 477.1 %all-gather.17.cloned.1.call-start = ((), (), s32[]{:S(2)}) async-start(), calls=%async_computation.7 | async-start | bytes 5242880 | tf_op jit(solution)/shard_map/all_gather | solution.py:658
  1338.4 567.9 %all-gather.23.cloned.1.call-start = ((), (), s32[]{:S(2)}) async-start(), calls=%async_computation.13 | async-start | bytes 10813440 | tf_op jit(solution)/shard_map/all_gather | solution.py:609
  1428.1 569.9 %all-gather.21.cloned.1.call-start = ((), (), s32[]{:S(2)}) async-start(), calls=%async_computation.11 | async-start | bytes 10813440 | tf_op jit(solution)/shard_map/all_gather | solution.py:609
  (383 other events, 5700.9 us)
Sparse Core Ops, SparseCore 0:
  18.8 66.3 all-gather.12
  87.4 169.6 all-gather.24
  258.7 62.3 all-gather.14
  323.1 169.7 all-gather.26
  987.2 77.9 reduce-scatter.6
  1196.7 79.1 reduce-scatter.4
  1278.9 149.1 reduce-scatter.10
  1431.0 149.4 reduce-scatter.8
  1586.6 118.3 all-reduce.1
  1706.6 53.4 all-gather.18
  1762.0 52.6 all-gather.16
  1816.5 89.7 all-gather.22
  1908.1 89.7 all-gather.20

commit v2 on v0

v2 whole, which is shorter than its diff:
```python
import functools

import jax
import jax.numpy as jnp
from jax import lax
from jax.experimental import pallas as pl
from jax.experimental.pallas import tpu as pltpu
from jax.sharding import PartitionSpec as P

norm_eps = 1e-06
domain_scale = (1.0, 0.5, 2.0)
F32 = jnp.float32
BF16 = jnp.bfloat16
LANES = 128
VMEM_LIMIT = 56 * 1024 * 1024


def high_bit(s):
    return 1 << (s.bit_length() - 1)


def low_bit(s):
    return s & -s


def swap_dp(v, bit):
    return lax.ppermute(v, "dp", [(i, i ^ bit) for i in range(lax.axis_size("dp"))])


def swap_core(v):
    return lax.ppermute(v, "mp", [(i, i ^ 1) for i in range(lax.axis_size("mp"))])


def slot_groups():
    slots = sorted(range(lax.axis_size("dp")), key=lambda s: (bin(s).count("1"), s))
    near = [s for s in slots if bin(s).count("1") <= 1]
    return near, slots[len(near) :]


def join(parts):
    return parts[0] if len(parts) == 1 else jnp.concatenate(parts, 0)


def plane_gather(x):
    near, far = slot_groups()
    half = x.shape[0] // 2
    slots = {0: x}
    for s in near[1:]:
        slots[s] = swap_dp(x, s)
    for s in far:
        top, low = high_bit(s), low_bit(s)
        slots[s] = join([swap_dp(slots[s ^ top][:half], top), swap_dp(slots[s ^ low][half:], low)])
    own = join([slots[s] for s in range(len(slots))])
    return [own, swap_core(own)]


def plane_scatter(own, other, product, first_fill=(), last_fill=()):
    near, far = slot_groups()
    count = own.shape[0] // lax.axis_size("dp")
    half = count // 2
    other = swap_core(product(other).astype(BF16))
    both = product(own) + other.astype(F32)
    total = {s: both[s * count : (s + 1) * count] for s in near + far}
    for s in reversed(far):
        top, low = high_bit(s), low_bit(s)
        first = swap_dp(total[s][:half].astype(BF16), top)
        last = swap_dp(total[s][half:].astype(BF16), low)
        if s == far[0]:
            first, last, first_fill = tie_all(first, last, first_fill)
        total[s ^ top] = join([total[s ^ top][:half] + first.astype(F32), total[s ^ top][half:]])
        total[s ^ low] = join([total[s ^ low][:half], total[s ^ low][half:] + last.astype(F32)])
    got = [swap_dp(total[s].astype(BF16), s) for s in near[1:]]
    got, last_fill = tie_all(got, last_fill)
    out = total[0]
    for v in got:
        out = out + v.astype(F32)
    return out, first_fill, last_fill


def plane_scatter_rows(totals):
    part = totals[:, 0] + swap_core(totals[:, 1])
    while part.shape[0] > 1:
        half = part.shape[0] // 2
        part = part[:half] + swap_dp(part[half:], half)
    return part[0]


def in_parts(vec):
    parts = []
    rest = vec
    for _ in range(3):
        part = lax.reduce_precision(rest, 8, 7)
        rest = rest - part
        parts.append(part.astype(BF16))
    return jnp.pad(jnp.stack(parts, 1), ((0, 0), (0, LANES - 3)))


def strip_halves(v):
    half = v.shape[1] // 32 * 16
    return v[0, :half], v[0, half:]


def strips_near(halves):
    near, _ = slot_groups()
    slots = {0: tuple(halves)}
    for s in near[1:]:
        slots[s] = tuple(swap_dp(v, s) for v in halves)
    return slots


def strips_far(slots):
    near, far = slot_groups()
    slots = dict(slots)
    for s in far:
        top, low = high_bit(s), low_bit(s)
        slots[s] = (swap_dp(slots[s ^ top][0], top), swap_dp(slots[s ^ low][1], low))
    return [slots[s] for s in range(len(slots))]


def in_columns(slots):
    slots = jnp.stack([jnp.concatenate(halves, 0) for halves in slots], 0)
    column = lax.axis_index("dp")
    return jnp.stack(
        [
            lax.dynamic_index_in_dim(slots, column ^ s, 0, keepdims=False)
            for s in range(slots.shape[0])
        ],
        0,
    )


def line_sum(v):
    size = lax.axis_size("mp")
    bit = 2
    while bit < size:
        v = v + lax.ppermute(v, "mp", [(i, i ^ bit) for i in range(size)])
        bit *= 2
    return v


def sum_all(v):
    v = v + swap_core(v)
    bit = 1
    while bit < lax.axis_size("dp"):
        v = v + swap_dp(v, bit)
        bit *= 2
    return line_sum(v)


def tie_all(*values):
    return lax.optimization_barrier(values)


def line_groups():
    size = lax.axis_size("mp")
    return [[place * 2 + core for place in range(size // 2)] for core in (0, 1)]


def line_gather(v):
    return lax.all_gather(v, "mp", axis=0, tiled=False, axis_index_groups=line_groups())


def line_scatter(v):
    return lax.psum_scatter(
        v, "mp", scatter_dimension=0, tiled=True, axis_index_groups=line_groups()
    )


def line_carry(decay, value, ahead):
    size = lax.axis_size("mp")
    packed = jnp.stack([decay, value], 0)
    total = None
    for step in reversed(range(1, size // 2)):
        pairs = [(i, i + 2 * step) for i in range(size - 2 * step)]
        if ahead:
            pairs = [(b, a) for a, b in pairs]
        got = lax.ppermute(packed, "mp", pairs)
        total = got[1] if total is None else got[1] + got[0] * total
    return jnp.zeros_like(value) if total is None else total


def in_order(core, own, other):
    return jnp.where(core == 0, own, other), jnp.where(core == 0, other, own)


def take(refs, count):
    return refs[:count], refs[count:]


class Places:
    def __init__(self, slots, rows):
        self.blocks, self.rows, self.half = 2 * slots, rows, rows // 2

    def __iter__(self):
        for block in range(self.blocks):
            for h in (0, 1):
                here = pl.ds(block * self.rows + h * self.half, self.half)
                part = pl.ds(block // 2 * self.half, self.half)
                yield block, h, here, 2 * h + block % 2, part


def scan_kernel(places, core_ref, *refs):
    pieces, rows = 4, places.rows
    inputs, refs = take(refs, pieces)
    forgets, refs = take(refs, pieces)
    bound_ref, local_ref, decay_ref, end_ref, full_ref, seq_end_ref, seq_full_ref = refs
    blocks = places.blocks
    low = bound_ref[...]
    for _, _, here, p, part in places:
        forget = low + (1.0 - low) * jax.nn.sigmoid(forgets[p][part, :])
        decay_ref[here, :] = forget
        local_ref[here, :] = (1.0 - forget) * jax.nn.silu(inputs[p][part, :])

    def step(t, kept):
        state, decay = kept
        place = pl.ds(t, blocks, stride=rows)
        forget = decay_ref[place, :]
        state = forget * state + local_ref[place, :]
        decay = forget * decay
        local_ref[place, :] = state
        decay_ref[place, :] = decay
        return state, decay

    none = decay_ref[pl.ds(0, blocks, stride=rows), :] * 0.0
    end, full = lax.fori_loop(0, rows, step, (none, none + 1.0), unroll=8)
    end_ref[...] = end
    full_ref[...] = full
    core = core_ref[0]
    own, other = pl.ds(0, blocks // 2, stride=2), pl.ds(1, blocks // 2, stride=2)
    end_a, end_b = in_order(core, end_ref[own, :], end_ref[other, :])
    full_a, full_b = in_order(core, full_ref[own, :], full_ref[other, :])
    seq_end_ref[...] = end_b + full_b * end_a
    seq_full_ref[...] = full_a * full_b


def state_kernel(places, core_ref, *refs):
    pieces = 4
    gates, refs = take(refs, pieces)
    local_ref, decay_ref, end_ref, full_ref, enter_ref, gain_ref = refs[:6]
    state_ref, square_ref, carry_ref = refs[6:9]
    outs = refs[9:]
    core = core_ref[0]
    slots = places.blocks // 2
    own, other = pl.ds(0, slots, stride=2), pl.ds(1, slots, stride=2)
    end_a, _ = in_order(core, end_ref[own, :], end_ref[other, :])
    full_a, _ = in_order(core, full_ref[own, :], full_ref[other, :])
    carry_a = enter_ref[...]
    carry_b = end_a + full_a * carry_a
    carry_own, carry_other = in_order(core, carry_a, carry_b)
    carry_ref[own, :] = carry_own
    carry_ref[other, :] = carry_other
    gain = gain_ref[...]
    for block, h, here, p, part in places:
        row = slice(block, block + 1)
        state = local_ref[here, :] + decay_ref[here, :] * carry_ref[row, :]
        state_ref[here, :] = state
        gated = state * jax.nn.silu(gates[p][part, :])
        outs[p][part, :] = (gated * gain).astype(BF16)
        total = jnp.sum((gated * gated).T, 0, keepdims=True)
        row = slice(h * places.blocks + block, h * places.blocks + block + 1)

        @pl.when(pl.program_id(0) == 0)
        def _(row=row, total=total):
            square_ref[row, :] = total

        @pl.when(pl.program_id(0) > 0)
        def _(row=row, total=total):
            square_ref[row, :] = square_ref[row, :] + total


def row_stat(parts):
    parts = parts.astype(F32)
    return (parts[:, 0:1] + parts[:, 1:2]) + parts[:, 2:3]


def scan_back_kernel(places, core_ref, *refs):
    pieces, rows = 4, places.rows
    grads, refs = take(refs, pieces)
    forgets, refs = take(refs, pieces)
    gates, refs = take(refs, pieces)
    stats, refs = take(refs, pieces)
    state_ref, bound_ref, gain_ref = refs[:3]
    local_ref, decay_ref, end_ref, full_ref, seq_end_ref, seq_full_ref, forget_ref = refs[3:]
    blocks = places.blocks
    low = bound_ref[...]
    gain = gain_ref[...]
    for _, _, here, p, part in places:
        silu_gate = jax.nn.silu(gates[p][part, :])
        gated = state_ref[here, :] * silu_gate
        stat = row_stat(stats[p][part, :])
        local_ref[here, :] = (grads[p][part, :] * gain - gated * stat) * silu_gate
        forget_ref[here, :] = low + (1.0 - low) * jax.nn.sigmoid(forgets[p][part, :])

    def step(k, kept):
        t = rows - 1 - k
        state, decay, forget = kept
        place = pl.ds(t, blocks, stride=rows)
        state = forget * state + local_ref[place, :]
        decay = forget * decay
        local_ref[place, :] = state
        decay_ref[place, :] = decay
        return state, decay, forget_ref[place, :]

    none = forget_ref[pl.ds(0, blocks, stride=rows), :] * 0.0
    state, decay, forget = lax.fori_loop(
        0, rows, step, (none, none + 1.0, none + 1.0), unroll=8
    )
    end_ref[...] = forget * state
    full_ref[...] = forget * decay
    core = core_ref[0]
    own, other = pl.ds(0, blocks // 2, stride=2), pl.ds(1, blocks // 2, stride=2)
    end_a, end_b = in_order(core, end_ref[own, :], end_ref[other, :])
    full_a, full_b = in_order(core, full_ref[own, :], full_ref[other, :])
    seq_end_ref[...] = end_a + full_a * end_b
    seq_full_ref[...] = full_a * full_b


def project_back_kernel(places, core_ref, *refs):
    pieces, half = 4, places.half
    grads, refs = take(refs, pieces)
    inputs, refs = take(refs, pieces)
    forgets, refs = take(refs, pieces)
    gates, refs = take(refs, pieces)
    stats, refs = take(refs, pieces)
    state_ref, bound_ref, gain_ref, carry_ref = refs[:4]
    local_ref, decay_ref, end_ref, full_ref, enter_ref = refs[4:9]
    outs, (bound_grad_ref, gain_grad_ref, back_ref) = take(refs[9:], pieces)
    core = core_ref[0]
    slots = places.blocks // 2
    width = outs[0].shape[1] // 3
    column = pl.program_id(0) * LANES
    own, other = pl.ds(0, slots, stride=2), pl.ds(1, slots, stride=2)
    _, end_b = in_order(core, end_ref[own, :], end_ref[other, :])
    _, full_b = in_order(core, full_ref[own, :], full_ref[other, :])
    carry_b = enter_ref[...]
    carry_a = end_b + full_b * carry_b
    carry_own, carry_other = in_order(core, carry_a, carry_b)
    back_ref[own, :] = carry_own
    back_ref[other, :] = carry_other
    low = bound_ref[...]
    gain = gain_ref[...]
    bound_total = jnp.zeros((1, LANES), F32)
    gain_total = jnp.zeros((1, LANES), F32)
    top = lax.broadcasted_iota(jnp.int32, (half, LANES), 0) == 0
    for block, h, here, p, part in places:
        row = slice(block, block + 1)
        state = state_ref[here, :]
        if h == 0:
            before = carry_ref[row, :]
        else:
            before = state_ref[pl.ds(block * places.rows + half - 1, 1), :]
        before = jnp.where(top, before, pltpu.roll(state, 1, 0))
        gate = gates[p][part, :]
        gate_sig = jax.nn.sigmoid(gate)
        silu_gate = gate * gate_sig
        grad = grads[p][part, :]
        gated = state * silu_gate
        dgated = grad * gain - gated * row_stat(stats[p][part, :])
        dstate = local_ref[here, :] + decay_ref[here, :] * back_ref[row, :]
        enter = inputs[p][part, :]
        enter_sig = jax.nn.sigmoid(enter)
        forget_sig = jax.nn.sigmoid(forgets[p][part, :])
        keep = (1.0 - low) * (1.0 - forget_sig)
        dforget = dstate * (before - enter * enter_sig)
        slope = dforget * (1.0 - forget_sig)
        made = (
            dstate * keep * enter_sig * (1.0 + enter * (1.0 - enter_sig)),
            slope * (1.0 - low) * forget_sig,
            dgated * state * gate_sig * (1.0 + gate * (1.0 - gate_sig)),
        )
        for which, value in enumerate(made):
            lanes = pl.ds(pl.multiple_of(which * width + column, LANES), LANES)
            outs[p][part, lanes] = value.astype(BF16)
        bound_total = bound_total + jnp.sum(slope, 0, keepdims=True)
        gain_total = gain_total + jnp.sum(grad * gated, 0, keepdims=True)
    bound_grad_ref[...] = bound_total
    gain_grad_ref[...] = gain_total


def struct(shape, dtype=F32):
    return jax.ShapeDtypeStruct(shape, dtype)


class Mixer:
    def __init__(self, core, projected, bound, gain):
        self.core, self.projected, self.bound, self.gain = core, projected, bound, gain
        self.total = sum(p.shape[0] for p in projected)
        self.blocks = 2 * lax.axis_size("dp")
        self.rows = self.total // self.blocks
        self.places = Places(lax.axis_size("dp"), self.rows)
        self.channels = projected[0].shape[1] // 3
        self.steps = self.channels // LANES

    def column(self, rows, offset=0):
        return pl.BlockSpec((rows, LANES), lambda i, offset=offset: (0, offset + i))

    def pieces(self, which=0):
        return [self.column(p.shape[0], which * self.steps) for p in self.projected]

    def whole(self, rows, columns):
        return pl.BlockSpec((rows, columns), lambda i: (0, 0))

    def scanned(self):
        sizes = [self.total] * 2 + [self.blocks] * 2 + [self.blocks // 2] * 2
        return [self.column(n) for n in sizes], [struct((n, self.channels)) for n in sizes]

    def call(self, body, name, in_specs, out_specs, out_shapes, scratch, flops, args):
        moved = 1024
        call = pl.pallas_call(
            functools.partial(body, self.places),
            name=name,
            grid=(self.steps,),
            in_specs=[pl.BlockSpec(memory_space=pltpu.SMEM)] + in_specs,
            out_specs=out_specs,
            out_shape=out_shapes,
            scratch_shapes=scratch,
            compiler_params=pltpu.CompilerParams(
                vmem_limit_bytes=VMEM_LIMIT, dimension_semantics=("arbitrary",)
            ),
            cost_estimate=pl.CostEstimate(
                flops=flops, bytes_accessed=moved, transcendentals=0
            ),
        )
        return list(call(self.core, *args))

    def scan(self):
        specs, shapes = self.scanned()
        return self.call(
            scan_kernel,
            "mixer_scan",
            self.pieces(0) + self.pieces(1) + [self.column(1)],
            specs,
            shapes,
            [],
            200,
            self.projected * 2 + [self.bound],
        )

    def state(self, scanned, enter):
        total, blocks, channels = self.total, self.blocks, self.channels
        sizes = [total] * 2 + [blocks] * 2 + [blocks // 2, 1]
        outs = self.call(
            state_kernel,
            "mixer_state",
            self.pieces(2) + [self.column(n) for n in sizes],
            [self.column(total), self.whole(2 * blocks, self.rows // 2), self.column(blocks)]
            + self.pieces(),
            [struct((total, channels)), struct((2 * blocks, self.rows // 2)), struct((blocks, channels))]
            + [struct((p.shape[0], channels), BF16) for p in self.projected],
            [],
            100,
            self.projected + scanned[:4] + [enter, self.gain],
        )
        return outs[0], outs[1], outs[2], list(outs[3:])

    def scan_back(self, grads, state, stats):
        specs, shapes = self.scanned()
        return self.call(
            scan_back_kernel,
            "mixer_scan_back",
            self.pieces()
            + self.pieces(1)
            + self.pieces(2)
            + [
                pl.BlockSpec((p.shape[0], LANES), lambda i, last=p.shape[1] // LANES - 1: (0, last))
                for p in stats
            ]
            + [self.column(self.total)]
            + [self.column(1)] * 2,
            specs,
            shapes,
            [pltpu.VMEM((self.total, LANES), F32)],
            250,
            grads + self.projected * 2 + stats + [state, self.bound, self.gain],
        )

    def project_back(self, grads, state, stats, carry, scanned, enter):
        total, blocks, channels = self.total, self.blocks, self.channels
        sizes = [1, 1, blocks, total, total, blocks, blocks, blocks // 2]
        outs = self.call(
            project_back_kernel,
            "mixer_project_back",
            self.pieces()
            + self.pieces(0)
            + self.pieces(1)
            + self.pieces(2)
            + [
                pl.BlockSpec((p.shape[0], LANES), lambda i, last=p.shape[1] // LANES - 1: (0, last))
                for p in stats
            ]
            + [self.column(total)]
            + [self.column(n) for n in sizes],
            [self.whole(*p.shape) for p in self.projected] + [self.column(1)] * 2,
            [struct(p.shape, BF16) for p in self.projected] + [struct((1, channels))] * 2,
            [pltpu.VMEM((blocks, LANES), F32)],
            200,
            grads
            + self.projected * 3
            + stats
            + [state, self.bound, self.gain, carry]
            + scanned[:4]
            + [enter],
        )
        return list(outs[:-2]), outs[-2], outs[-1]


def matmul(a, b):
    return jnp.dot(a, b, preferred_element_type=F32)


def matmul_t(a, b):
    return lax.dot_general(a, b, (((1,), (1,)), ((), ())), preferred_element_type=F32)


def matmul_rows(a, b):
    return lax.dot_general(a, b, (((0,), (0,)), ((), ())), preferred_element_type=F32)


def rows_product(a, b):
    return matmul_rows(join(a), join(b)).astype(BF16)


@jax.tree_util.register_pytree_node_class
class Pair:
    def __init__(self, a, b):
        self.a, self.b = a, b

    @property
    def shape(self):
        return self.a.shape

    def __getitem__(self, part):
        return Pair(self.a[part], self.b[part])

    def tree_flatten(self):
        return (self.a, self.b), None

    @classmethod
    def tree_unflatten(cls, _, parts):
        return cls(*parts)


def rms_factor(values):
    return lax.rsqrt(jnp.mean(values * values, -1, keepdims=True) + norm_eps)


def rms_back(values, gain, grad):
    factor = rms_factor(values)
    normed = values * factor
    scaled = grad * gain
    back = factor * (scaled - normed * jnp.mean(scaled * normed, -1, keepdims=True))
    return back, jnp.sum(grad * normed, 0)


def bound_rows(logits):
    return jnp.cumsum(jax.nn.softmax(logits, 0), 0)


def local(
    hidden_in,
    cotangent,
    domain_tags,
    mix_weight,
    mix_out_weight,
    glu_weight,
    glu_out_weight,
    mix_gain,
    out_gain,
    glu_gain,
    bound_logits,
):
    dp = lax.axis_size("dp")
    line = lax.axis_size("mp") // 2
    column = lax.axis_index("dp")
    member = lax.axis_index("mp")
    core = member % 2
    core_arg = core.astype(jnp.int32).reshape(1)
    width = hidden_in.shape[1]
    layers = mix_weight.shape[0]
    channels = mix_weight.shape[3]
    units = glu_weight.shape[3]
    c_strip, u_strip = channels // dp, units // dp

    def cut(array, axis, size):
        return lax.dynamic_slice_in_dim(array, column * size, size, axis)

    scale_table = jnp.array(domain_scale, dtype=F32)
    match = domain_tags[0] == jnp.arange(3, dtype=jnp.int32)
    grad = cotangent.astype(F32) * jnp.sum(jnp.where(match, scale_table, 0.0))
    bound_vals, bound_back = jax.vjp(bound_rows, bound_logits)

    mix_w, out_w, gate_w, up_w, down_w = ([None] * layers for _ in range(5))

    def mix_strip(weight, out=None):
        strip = cut(weight, 2, c_strip).transpose(1, 2, 0).reshape(3 * c_strip, width)
        return strip if out is None else jnp.concatenate([strip, cut(out, 0, c_strip)], 0)

    def glu_strip(weight):
        return cut(weight, 2, u_strip).transpose(1, 2, 0).reshape(2 * u_strip, width)

    def gather_mix(l, strip, out=None):
        got = line_gather(strip)
        mixes = got[:, : 3 * c_strip].reshape(line, 3, c_strip, width).transpose(1, 0, 2, 3)
        mix_w[l] = mixes.reshape(3 * line * c_strip, width)
        out = got[:, 3 * c_strip :] if out is None else line_gather(out)
        out_w[l] = out.reshape(line * c_strip, width)

    def gather_glu(l, strip):
        got = line_gather(strip)
        gate_w[l] = got[:, :u_strip].reshape(line * u_strip, width)
        up_w[l] = got[:, u_strip:].reshape(line * u_strip, width)

    def gather_down(l, strip):
        down_w[l] = line_gather(strip).reshape(line * u_strip, width)

    strip = mix_strip(mix_weight[0])
    strip, hidden_in, out_strip = tie_all(strip, hidden_in, mix_out_weight[0])
    gather_mix(0, strip, cut(out_strip, 0, c_strip))
    half = hidden_in.shape[0] // 2

    def halves(rows):
        return [rows[:half], rows[half:]]

    def gathered(lows):
        return [piece for low in lows for piece in plane_gather(low)]

    def normed(rows, gain):
        return (rows * rms_factor(rows) * gain).astype(BF16)

    grad = halves(grad)
    stream = halves(hidden_in.astype(F32))
    kept = []
    for l in range(layers):
        stream_in = stream
        lows = [normed(rows, mix_gain[l]) for rows in stream]
        if l == 0:
            small = jnp.concatenate([cut(bound_vals, 1, c_strip), cut(out_gain, 1, c_strip)], 0)
            lows, small, first_glu = tie_all(lows, small, glu_weight[0])
            strip, down = tie_all(glu_strip(first_glu), glu_out_weight[0])
            gather_glu(0, strip)
            down_strip = cut(down, 0, u_strip)
            small = lax.dynamic_update_slice(
                jnp.zeros((small.shape[0], line, c_strip), F32), small[:, None], (0, member // 2, 0)
            )
            small = line_sum(small).reshape(-1, line * c_strip)
            bounds = [small[i : i + 1] for i in range(layers)]
            gains = [small[bound_vals.shape[0] + i :][:1] for i in range(layers)]
        mixer_in = gathered(lows)
        projected = [matmul_t(rows, mix_w[l]) for rows in mixer_in]
        mixer = Mixer(core_arg, projected, bounds[l], gains[l])
        scanned = mixer.scan()
        enter = line_carry(scanned[5], scanned[4], False)
        state, squares, carry, mixed = mixer.state(scanned, enter)
        if l + 1 < layers:
            down_strip, *raws = tie_all(
                down_strip, mix_weight[l + 1], mix_out_weight[l + 1], glu_weight[l + 1]
            )
            gather_down(l, down_strip)
            strip, raw = tie_all(mix_strip(*raws[:2]), raws[2])
            gather_mix(l + 1, strip)
            strip, down = tie_all(glu_strip(raw), glu_out_weight[l + 1])
            gather_glu(l + 1, strip)
            down_strip = cut(down, 0, u_strip)
        else:
            gather_down(l, down_strip)
        squares = plane_scatter_rows(
            squares.reshape(2, dp, 2, half).transpose(1, 2, 0, 3).reshape(dp, 2, 2 * half)
        )
        out_factor = halves(lax.rsqrt(squares / width + norm_eps)[:, None])
        raw = [
            plane_scatter(*mixed[2 * h : 2 * h + 2], lambda rows, w=out_w[l]: matmul(rows, w))[0]
            for h in (0, 1)
        ]
        stream_mid = [a + b * c for a, b, c in zip(stream, raw, out_factor)]
        glu_in = gathered([normed(rows, glu_gain[l]) for rows in stream_mid])

        def glu(rows):
            a, b = matmul_t(rows, gate_w[l]), matmul_t(rows, up_w[l])
            return a, b, (jax.nn.silu(a) * b).astype(BF16)

        if l == 0:
            glu_in, grad_low = tie_all(glu_in, [rows.astype(BF16) for rows in grad])
            last_grad = gathered(grad_low)
        gate, up, hidden = zip(*[glu(rows) for rows in glu_in])
        if l == 0:
            hidden, last_grad = tie_all(hidden, last_grad)
        stream = [
            stream_mid[h]
            + plane_scatter(*hidden[2 * h : 2 * h + 2], lambda rows, w=down_w[l]: matmul(rows, w))[0]
            for h in (0, 1)
        ]
        kept.append(
            (
                stream_in,
                mixer_in,
                mixer,
                state,
                carry,
                mixed,
                out_factor,
                raw,
                stream_mid,
                glu_in,
                gate,
                up,
                hidden,
            )
        )

    mix_gain_parts = [None] * layers
    glu_gain_parts = [None] * layers
    out_gain_parts = [None] * layers
    bound_parts = [None] * layers

    grads = {}

    def place(name, l, value):
        if name not in grads:
            grads[name] = jnp.zeros((layers,) + value.shape, F32)
        grads[name] = lax.dynamic_update_index_in_dim(grads[name], value.astype(F32), l, 0)

    def finish_glu(l, slots):
        strips = in_columns(slots)
        place("glu_out", l, strips[:, :u_strip].reshape(units, width))
        strips = strips[:, u_strip:].reshape(dp, 2, u_strip, width).transpose(3, 1, 0, 2)
        place("glu", l, strips.reshape(width, 2, units))

    def finish_mix(l, slots):
        strips = in_columns(slots)
        place("mix_out", l, strips[:, 3 * c_strip :].reshape(channels, width))
        strips = strips[:, : 3 * c_strip].reshape(dp, 3, c_strip, width).transpose(3, 1, 0, 2)
        place("mix", l, strips.reshape(width, 3, channels))

    for l in reversed(range(layers)):
        (
            stream_in,
            mixer_in,
            mixer,
            state,
            carry,
            mixed,
            out_factor,
            raw,
            stream_mid,
            glu_in,
            gate,
            up,
            hidden,
        ) = kept[l]
        if l == layers - 1:
            down_grad = last_grad
        else:
            down_grad = gathered([rows.astype(BF16) for rows in grad])
            down_grad, glu_sum = tie_all(down_grad, glu_sum)
            glu_strips = strips_near(glu_sum)

        def glu_back(rows, a, b):
            dhidden = matmul_t(rows, down_w[l])
            sig = jax.nn.sigmoid(a)
            dgate = (dhidden * b * sig * (1.0 + a * (1.0 - sig))).astype(BF16)
            return Pair(dgate, (dhidden * a * sig).astype(BF16))

        def glu_product(rows):
            return matmul(rows.a, gate_w[l]) + matmul(rows.b, up_w[l])

        pairs = [glu_back(*args) for args in zip(down_grad, gate, up)]
        back_first, _, _ = plane_scatter(*pairs[:2], glu_product)
        fill = (
            rows_product([p.a for p in pairs], glu_in),
            rows_product([p.b for p in pairs], glu_in),
        )
        if l < layers - 1:
            fill += (glu_strips,)
        back_last, down_part, fill = plane_scatter(
            *pairs[2:], glu_product, rows_product(hidden, down_grad), fill
        )
        gate_part, up_part = fill[:2]
        if l < layers - 1:
            glu_strips = fill[2]
        sent = [v.reshape(line, u_strip, width) for v in (down_part, gate_part, up_part)]
        sent = jnp.concatenate(sent, 1)
        back, gain_part = zip(
            *[rms_back(v, glu_gain[l], d) for v, d in zip(stream_mid, (back_first, back_last))]
        )
        glu_gain_parts[l] = sum(gain_part)
        grad = [a + b for a, b in zip(grad, back)]
        if l < layers - 1:
            sent, summed = tie_all(sent, summed)
        glu_sum = strip_halves(line_scatter(sent))

        lows = []
        for rows, factor, y in zip(grad, out_factor, raw):
            low = (rows * factor).astype(BF16)
            stat = jnp.mean(low.astype(F32) * y, -1) * (factor * factor)[:, 0]
            lows.append(jnp.concatenate([low, in_parts(stat)], 1))
        out_grad = gathered(lows)
        if l < layers - 1:
            out_grad, summed, glu_strips = tie_all(out_grad, summed, glu_strips)
            glu_strips = strips_far(glu_strips)
            mix_strips = strips_far(strips_near(summed))
        padded = jnp.pad(out_w[l], ((0, 0), (0, LANES)))
        mixed_grad = [matmul_t(rows, padded) for rows in out_grad]
        scanned = mixer.scan_back(mixed_grad, state, out_grad)
        enter = line_carry(scanned[5], scanned[4], True)
        proj_grad, bound_parts[l], out_gain_parts[l] = mixer.project_back(
            mixed_grad, state, out_grad, carry, scanned, enter
        )
        out_part = rows_product(mixed, out_grad)[:, :width]
        mix_part = rows_product(proj_grad, mixer_in)

        def mix_sent(out_part, mix_part):
            mix_part = mix_part.reshape(3, line, c_strip, width).transpose(1, 0, 2, 3)
            mix_part = mix_part.reshape(line, 3 * c_strip, width)
            return jnp.concatenate([mix_part, out_part.reshape(line, c_strip, width)], 1)

        def mix_product(rows):
            return matmul(rows, mix_w[l])

        if l == 0:
            proj_grad, sent = tie_all(proj_grad, mix_sent(out_part, mix_part))
            back_first, glu_sum, _ = plane_scatter(*proj_grad[:2], mix_product, glu_sum)
            back_last, _, (glu_strips, mix_strips) = plane_scatter(
                *proj_grad[2:], mix_product, (), (glu_strips, mix_strips)
            )
            finish_glu(1, glu_strips)
            finish_mix(1, mix_strips)
        else:
            back_first, _, _ = plane_scatter(*proj_grad[:2], mix_product)
            back_last, out_part, mix_part = plane_scatter(
                *proj_grad[2:], mix_product, out_part, mix_part
            )
            sent = mix_sent(out_part, mix_part)
        back, gain_part = zip(
            *[rms_back(v, mix_gain[l], d) for v, d in zip(stream_in, (back_first, back_last))]
        )
        mix_gain_parts[l] = sum(gain_part)
        grad = [a + b for a, b in zip(grad, back)]
        sent, glu_sum = tie_all(sent, glu_sum)
        summed = strip_halves(line_scatter(sent))
    finish_glu(0, strips_far(strips_near(glu_sum)))
    finish_mix(0, strips_far(strips_near(summed)))

    def spread(row):
        zeros = jnp.zeros((line, 2, dp, c_strip), F32)
        return lax.dynamic_update_slice(
            zeros, row.reshape(line, 1, 1, c_strip), (0, core, column, 0)
        ).reshape(-1)

    rows = jnp.stack(
        mix_gain_parts
        + glu_gain_parts
        + [spread(v) for v in out_gain_parts]
        + [spread(v) for v in bound_parts]
    )
    rows = sum_all(rows)
    mix_gain_grad = rows[:layers]
    glu_gain_grad = rows[layers : 2 * layers]
    mine = lax.dynamic_slice_in_dim(rows[2 * layers :], member * channels, channels, 1)
    out_gain_grad = mine[:layers]
    extra = jnp.zeros((bound_vals.shape[0] - layers, channels), F32)
    bound_grad = bound_back(jnp.concatenate([mine[layers:], extra], 0))[0]
    return (
        jnp.concatenate(stream, 0),
        jnp.concatenate(grad, 0),
        grads["mix"],
        grads["mix_out"],
        grads["glu"],
        grads["glu_out"],
        mix_gain_grad,
        out_gain_grad,
        glu_gain_grad,
        bound_grad,
    )


def solution(mesh):
    return jax.shard_map(
        local,
        mesh=mesh,
        in_specs=(
            P(("dp", "mp"), None),
            P(("dp", "mp"), None),
            P("dp"),
            P(None, None, None, "mp"),
            P(None, "mp", None),
            P(None, None, None, "mp"),
            P(None, "mp", None),
            P(),
            P(None, "mp"),
            P(),
            P(None, "mp"),
        ),
        out_specs=(
            P(("dp", "mp"), None),
            P(("dp", "mp"), None),
            P(None, None, None, "mp"),
            P(None, "mp", None),
            P(None, None, None, "mp"),
            P(None, "mp", None),
            P(),
            P(None, "mp"),
            P(),
            P(None, "mp"),
        ),
        check_vma=False,
    )
```

time: 2810 us -> 1510 us (0.54)
  waiting for transfers between devices: 1600 us -> 476 us
  local copies, waits for them, and re-layouts: 506 us -> 232 us
  starting transfers between devices: 1.58 us -> 223 us
  other arithmetic: 255 us -> 139 us
  blocking collectives: 116 us -> 0 us
  Pallas kernels: 0 us -> 79.7 us
  matrix products: 291 us -> 332 us
    all_gather x8 -> x7, waiting for transfers between devices: 610 us -> 0.03 us  [line_gather(): lax.all_gather(v, 'mp', axis=0, tiled=False, axis_index_groups=line_group...]
    reduce_scatter x8 -> x4, waiting for transfers between devices: 603 us -> 0.01 us  [line_scatter(): lax.psum_scatter(v, 'mp', scatter_dimension=0, tiled=True, axis_index_gro...]
    ppermute x0 -> x209, waiting for transfers between devices: none -> 476 us  [the longest x158 451 us: swap_dp(): lax.ppermute(v, 'dp', [(i, i ^ bit) for i in range(lax.axis_size('dp'))])]
    psum x1 -> x0, waiting for transfers between devices: 391 us -> none  [local(): lax.psum(jnp.stack(mix_grads).astype(jnp.bfloat16), 'dp')]
    pad x176 -> x0, local copies, waits for them, and re-layouts: 261 us -> none  [recurrence(): lax.associative_scan(combine, (forget.reshape(seq_shape), update.reshape(...]
    ppermute x0 -> x209, starting transfers between devices: none -> 210 us  [the longest x158 169 us: swap_dp(): lax.ppermute(v, 'dp', [(i, i ^ bit) for i in range(lax.axis_size('dp'))])]
    slice x180 -> x79, local copies, waits for them, and re-layouts: 201 us -> 40.5 us  [the longest x2 7.64 us: gather_glu(): gate_w[l] = got[:, :u_strip].reshape(line * u_strip, width)]
    psum x6 -> x0, blocking collectives: 116 us -> none  [the longest x1 38.3 us: local(): lax.psum((jnp.stack(mix_gain_parts), jnp.stack(glu_gain_parts)), ('dp', '...]
  transfers between devices with their start and end apart: 17 -> 220, of which waited for: 16 -> 108; matrix products, arithmetic and copies ran while one was open for 6% -> 41% of each run, Pallas kernels for 0% -> 5%
where the time goes in v2:
time: 1510 us; the launch traced here: 1500 us
  waiting for transfers between devices  476 us (32%)
  matrix products  332 us (22%)
  local copies, waits for them, and re-layouts  232 us (15%)
  starting transfers between devices  223 us (15%)
  other arithmetic  139 us (9%)
  Pallas kernels  79.7 us (5%)
  between operations  19.4 us (1%)
    ppermute x158, waiting for transfers between devices, swap_dp(): lax.ppermute(v, 'dp', [(i, i ^ bit) for i in range(lax.axis_size('dp'))])  451 us
    ppermute x158, starting transfers between devices, swap_dp(): lax.ppermute(v, 'dp', [(i, i ^ bit) for i in range(lax.axis_size('dp'))])  169 us
    dot_general x40, matrix products, matmul_t(): lax.dot_general(a, b, (((1,), (1,)), ((), ())), preferred_element_type=F32)  139 us
    unnamed x586, local copies, waits for them, and re-layouts  110 us
    dot_general x40, matrix products, matmul(): return jnp.dot(a, b, preferred_element_type=F32)  106 us
    dot_general x10, matrix products, matmul_rows(): lax.dot_general(a, b, (((0,), (0,)), ((), ())), preferred_element_type=F32)  87.6 us
    pallas_call x8, Pallas kernels, call(): return list(call(self.core, *args))  79.7 us
  transfers between devices with their start and end apart: 220, of which 108 were waited for; matrix products, arithmetic and copies ran while one was open for 41% of the time, Pallas kernels for 5%

profile of v2, /device:TPU:0, one launch (start us, length us, event | category | flops | bytes accessed | tf_op | source)
XLA Modules:
  0.0 1502.1 jit_solution(14142112607348407905)
XLA Ops:
  21.3 11.2 slice_bitcast_fusion
  65.2 12.3 collective-permute-done.6
  121.5 9.1 mixer_scan.2
  165.7 12.1 all-gather.23.cloned.1.call-start
  225.5 9.6 collective-permute-done.34
  237.4 9.6 collective-permute-done.23
  373.1 10.6 collective-permute-done.54
  394.7 11.9 collective-permute-done.61
  412.9 10.3 collective-permute-done.64
  652.1 10.6 fusion.27
  665.2 11.1 convolution_convert_fusion.5
  738.3 11.1 collective-permute-done.109
  802.5 14.6 mixer_scan_back.2
  829.1 9.2 mixer_project_back.2
  868.7 9.4 convolution_convert_fusion.1
  896.8 10.6 collective-permute-done.133
  910.0 9.7 collective-permute-done.142
  970.9 10.3 fusion.24
  1023.3 11.5 collective-permute-done.150
  1036.7 11.3 convolution_convert_fusion.3
  1048.0 10.6 collective-permute-done.163
  1132.7 14.6 mixer_scan_back.3
  1159.6 9.3 mixer_project_back.3
  1168.9 10.9 convolution_convert_fusion
  1223.8 10.0 collective-permute-done.189
  1235.9 9.1 collective-permute-done.190
  1253.4 19.1 %collective-permute-done.191 = bf16[128,2048]{1,0:T(8,128)(2,1)S(1)} collective-permute-done((bf16[128,2048]{1,0:T(8,128)(2,1)S(1)}, bf16[128,2048]{1,0:T(8,128)(2,1)S(1)}, u32[]{:S(2)}, u32[]{:S(2)}) %collective-permute-start.191) | collective-permute-done | bytes 524320 | tf_op jit(solution)/shard_map/ppermute | solution.py:27
  1274.4 9.3 collective-permute-done.182
  1347.8 34.2 %collective-permute-done.205 = f32[8,2048]{1,0:T(8,128)S(1)} collective-permute-done((f32[8,2048]{1,0:T(8,128)S(1)}, f32[8,2048]{1,0:T(8,128)S(1)}, u32[]{:S(2)}, u32[]{:S(2)}) %collective-permute-start.205) | collective-permute-done | bytes 65568 | tf_op jit(solution)/shard_map/ppermute | solution.py:27
  1404.2 13.3 collective-permute-done.202
  1456.3 9.0 collective-permute-done.194
  1480.4 12.7 copy.121
  (1441 shorter events, 1104.6 us)
Async XLA Ops:
  7.2 92.4 %all-gather.15.cloned.1.call-start = ((), (), s32[]{:S(2)}) async-start(), calls=%async_computation.8 | async-start | bytes 3932160 | tf_op jit(solution)/shard_map/all_gather | solution.py:160
  19.4 130.5 %all-gather.17.cloned.1.call-start = ((), (), s32[]{:S(2)}) async-start(), calls=%async_computation.9 | async-start | bytes 1310720 | tf_op jit(solution)/shard_map/all_gather | solution.py:160
  38.8 226.8 %all-gather.19.cloned.1.call-start = ((), (), s32[]{:S(2)}) async-start(), calls=%async_computation.10 | async-start | bytes 7208960 | tf_op jit(solution)/shard_map/all_gather | solution.py:160
  62.7 265.6 %all-gather.21.cloned.1.call-start = ((), (), s32[]{:S(2)}) async-start(), calls=%async_computation.11 | async-start | bytes 3604480 | tf_op jit(solution)/shard_map/all_gather | solution.py:160
  165.7 270.5 %all-gather.23.cloned.1.call-start = ((), (), s32[]{:S(2)}) async-start(), calls=%async_computation.12 | async-start | bytes 5242880 | tf_op jit(solution)/shard_map/all_gather | solution.py:160
  259.7 234.8 %all-gather.25.cloned.1.call-start = ((), (), s32[]{:S(2)}) async-start(), calls=%async_computation.13 | async-start | bytes 7208960 | tf_op jit(solution)/shard_map/all_gather | solution.py:160
  345.8 222.3 %all-gather.27.cloned.1.call-start = ((), (), s32[]{:S(2)}) async-start(), calls=%async_computation.14 | async-start | bytes 3604480 | tf_op jit(solution)/shard_map/all_gather | solution.py:160
  489.1 453.4 %reduce-scatter.5.cloned.1.call-start = ((), (), s32[]{:S(2)}) async-start(), calls=%async_computation.4 | async-start | bytes 10813440 | tf_op jit(solution)/shard_map/reduce_scatter | solution.py:164
  631.6 46.6 %collective-permute-start.107 = (bf16[128,2048]{1,0:T(8,128)(2,1)}, bf16[128,2048]{1,0:T(8,128)(2,1)S(1)}, u32[]{:S(2)}, u32[]{:S(2)}) collective-permute-start(bf16[128,2048]{1,0:T(8,128)(2,1)} %pad_maximum_fusion.35), channel_id=1, source_target_pairs={{0,8},{8,0},{16,24},{24,16},{1,9},{9,1},{17,25},{25,17},{2,10},{10... | collective-permute-start | bytes 1572872 | tf_op jit(solution)/shard_map/ppermute | solution.py:27
  634.2 44.6 %collective-permute-start.108 = (bf16[128,2048]{1,0:T(8,128)(2,1)}, bf16[128,2048]{1,0:T(8,128)(2,1)}, u32[]{:S(2)}, u32[]{:S(2)}) collective-permute-start(bf16[128,2048]{1,0:T(8,128)(2,1)} %pad_maximum_fusion.36), channel_id=1, source_target_pairs={{0,16},{8,24},{16,0},{24,8},{1,17},{9,25},{17,1},{25,9},{2,18},{10... | collective-permute-start | bytes 1572872 | tf_op jit(solution)/shard_map/ppermute | solution.py:27
  636.9 41.9 %collective-permute-start.87 = (bf16[128,2048]{1,0:T(8,128)(2,1)}, bf16[128,2048]{1,0:T(8,128)(2,1)}, u32[]{:S(2)}, u32[]{:S(2)}) collective-permute-start(bf16[128,2048]{1,0:T(8,128)(2,1)} %pad_maximum_fusion.29), channel_id=1, source_target_pairs={{0,8},{8,0},{16,24},{24,16},{1,9},{9,1},{17,25},{25,17},{2,10},{10... | collective-permute-start | bytes 1572872 | tf_op jit(solution)/shard_map/ppermute | solution.py:27
  639.8 39.0 %collective-permute-start.88 = (bf16[128,2048]{1,0:T(8,128)(2,1)}, bf16[128,2048]{1,0:T(8,128)(2,1)}, u32[]{:S(2)}, u32[]{:S(2)}) collective-permute-start(bf16[128,2048]{1,0:T(8,128)(2,1)} %pad_maximum_fusion.30), channel_id=1, source_target_pairs={{0,16},{8,24},{16,0},{24,8},{1,17},{9,25},{17,1},{25,9},{2,18},{10... | collective-permute-start | bytes 1572872 | tf_op jit(solution)/shard_map/ppermute | solution.py:27
  775.8 338.2 %reduce-scatter.7.cloned.1.call-start = ((), (), s32[]{:S(2)}) async-start(), calls=%async_computation.5 | async-start | bytes 5242880 | tf_op jit(solution)/shard_map/reduce_scatter | solution.py:164
  947.3 74.8 %collective-permute-start.164 = (bf16[256,2048]{1,0:T(8,128)(2,1)}, bf16[256,2048]{1,0:T(8,128)(2,1)}, u32[]{:S(2)}, u32[]{:S(2)}) collective-permute-start(bf16[256,2048]{1,0:T(8,128)(2,1)} %slice_bitcast_fusion.7), channel_id=1, source_target_pairs={{0,16},{8,24},{16,0},{24,8},{1,17},{9,25},{17,1},{25,9},{2,18},{10... | collective-permute-start | bytes 3145736 | tf_op jit(solution)/shard_map/ppermute | solution.py:27
  948.3 99.7 %collective-permute-start.162 = (bf16[256,2048]{1,0:T(8,128)(2,1)}, bf16[256,2048]{1,0:T(8,128)(2,1)}, u32[]{:S(2)}, u32[]{:S(2)}) collective-permute-start(bf16[256,2048]{1,0:T(8,128)(2,1)} %slice_bitcast_fusion.7), channel_id=1, source_target_pairs={{0,8},{8,0},{16,24},{24,16},{1,9},{9,1},{17,25},{25,17},{2,10},{10... | collective-permute-start | bytes 3145736 | tf_op jit(solution)/shard_map/ppermute | solution.py:27
  949.8 355.6 %reduce-scatter.9.cloned.1.call-start = ((), (), s32[]{:S(2)}) async-start(), calls=%async_computation.6 | async-start | bytes 10813440 | tf_op jit(solution)/shard_map/reduce_scatter | solution.py:164
  950.0 98.0 %collective-permute-start.165 = (bf16[272,2048]{1,0:T(8,128)(2,1)}, bf16[272,2048]{1,0:T(8,128)(2,1)S(1)}, u32[]{:S(2)}, u32[]{:S(2)}) collective-permute-start(bf16[272,2048]{1,0:T(8,128)(2,1)} %slice_bitcast_fusion.5), channel_id=1, source_target_pairs={{0,16},{8,24},{16,0},{24,8},{1,17},{9,25},{17,1},{25,9},{2,18},{10... | collective-permute-start | bytes 3342344 | tf_op jit(solution)/shard_map/ppermute | solution.py:27
  961.4 40.4 %collective-permute-start.147 = (bf16[512,2048]{1,0:T(8,128)(2,1)}, bf16[512,2048]{1,0:T(8,128)(2,1)S(1)}, u32[]{:S(2)}, u32[]{:S(2)}) collective-permute-start(bf16[512,2048]{1,0:T(8,128)(2,1)} %add_convert_fusion.1), channel_id=1, source_target_pairs={{0,1},{1,0},{2,3},{3,2},{4,5},{5,4},{6,7},{7,6},{8,9},{9,8},{10,11... | collective-permute-start | bytes 6291464 | tf_op jit(solution)/shard_map/ppermute | solution.py:31
  1022.0 36.6 %collective-permute-start.163 = (bf16[272,2048]{1,0:T(8,128)(2,1)S(1)}, bf16[272,2048]{1,0:T(8,128)(2,1)S(1)}, u32[]{:S(2)}, u32[]{:S(2)}) collective-permute-start(bf16[272,2048]{1,0:T(8,128)(2,1)S(1)} %copy-done.72), channel_id=1, source_target_pairs={{0,8},{8,0},{16,24},{24,16},{1,9},{9,1},{17,25},{25,17},{2,10},{10... | collective-permute-start | bytes 3342344 | tf_op jit(solution)/shard_map/ppermute | solution.py:27
  1116.5 321.4 %reduce-scatter.11.cloned.1.call-start = ((), (), s32[]{:S(2)}) async-start(), calls=%async_computation.7 | async-start | bytes 5242880 | tf_op jit(solution)/shard_map/reduce_scatter | solution.py:164
  1194.6 52.1 %collective-permute-start.174 = (bf16[512,2048]{1,0:T(8,128)(2,1)}, bf16[512,2048]{1,0:T(8,128)(2,1)}, u32[]{:S(2)}, u32[]{:S(2)}) collective-permute-start(bf16[512,2048]{1,0:T(8,128)(2,1)} %convolution_convert_fusion.11), channel_id=1, source_target_pairs={{0,1},{1,0},{2,3},{3,2},{4,5},{5,4},{6,7},{7,6},{8,9},{9,8},{10,11... | collective-permute-start | bytes 6291464 | tf_op jit(solution)/shard_map/ppermute | solution.py:31
  1222.6 51.5 %collective-permute-start.184 = (bf16[256,2048]{1,0:T(8,128)(2,1)}, bf16[256,2048]{1,0:T(8,128)(2,1)S(1)}, u32[]{:S(2)}, u32[]{:S(2)}) collective-permute-start(bf16[256,2048]{1,0:T(8,128)(2,1)} %collective-permute-done.162), channel_id=1, source_target_pairs={{0,16},{8,24},{16,0},{24,8},{1,17},{9,25},{17,1},{25,9},{2,18},{10... | collective-permute-start | bytes 3145736 | tf_op jit(solution)/shard_map/ppermute | solution.py:27
  1233.8 40.6 %collective-permute-start.185 = (bf16[272,2048]{1,0:T(8,128)(2,1)S(1)}, bf16[272,2048]{1,0:T(8,128)(2,1)S(1)}, u32[]{:S(2)}, u32[]{:S(2)}) collective-permute-start(bf16[272,2048]{1,0:T(8,128)(2,1)S(1)} %copy-done.128), channel_id=1, source_target_pairs={{0,8},{8,0},{16,24},{24,16},{1,9},{9,1},{17,25},{25,17},{2,10},{10... | collective-permute-start | bytes 3342344 | tf_op jit(solution)/shard_map/ppermute | solution.py:27
  1235.4 37.1 %collective-permute-start.191 = (bf16[128,2048]{1,0:T(8,128)(2,1)S(1)}, bf16[128,2048]{1,0:T(8,128)(2,1)S(1)}, u32[]{:S(2)}, u32[]{:S(2)}) collective-permute-start(bf16[128,2048]{1,0:T(8,128)(2,1)S(1)} %collective-permute-done.189), channel_id=1, source_target_pairs={{0,8},{8,0},{16,24},{24,16},{1,9},{9,1},{17,25},{25,17},{2,10},{10... | collective-permute-start | bytes 1572872 | tf_op jit(solution)/shard_map/ppermute | solution.py:27
  1245.0 38.7 %collective-permute-start.182 = (bf16[128,2048]{1,0:T(8,128)(2,1)S(1)}, bf16[128,2048]{1,0:T(8,128)(2,1)S(1)}, u32[]{:S(2)}, u32[]{:S(2)}) collective-permute-start(bf16[128,2048]{1,0:T(8,128)(2,1)S(1)} %pad_maximum_fusion.49), channel_id=1, source_target_pairs={{0,8},{8,0},{16,24},{24,16},{1,9},{9,1},{17,25},{25,17},{2,10},{10... | collective-permute-start | bytes 1572872 | tf_op jit(solution)/shard_map/ppermute | solution.py:27
  1246.6 37.1 %collective-permute-start.183 = (bf16[128,2048]{1,0:T(8,128)(2,1)S(1)}, bf16[128,2048]{1,0:T(8,128)(2,1)}, u32[]{:S(2)}, u32[]{:S(2)}) collective-permute-start(bf16[128,2048]{1,0:T(8,128)(2,1)S(1)} %pad_maximum_fusion.50), channel_id=1, source_target_pairs={{0,16},{8,24},{16,0},{24,8},{1,17},{9,25},{17,1},{25,9},{2,18},{10... | collective-permute-start | bytes 1572872 | tf_op jit(solution)/shard_map/ppermute | solution.py:27
  1272.5 37.6 %collective-permute-start.176 = (bf16[64,2048]{1,0:T(8,128)(2,1)}, bf16[64,2048]{1,0:T(8,128)(2,1)}, u32[]{:S(2)}, u32[]{:S(2)}) collective-permute-start(bf16[64,2048]{1,0:T(8,128)(2,1)} %get-tuple-element.636), channel_id=1, source_target_pairs={{0,8},{8,0},{16,24},{24,16},{1,9},{9,1},{17,25},{25,17},{2,10},{10... | collective-permute-start | bytes 786440 | tf_op jit(solution)/shard_map/ppermute | solution.py:27
  1274.1 36.0 %collective-permute-start.175 = (bf16[64,2048]{1,0:T(8,128)(2,1)}, bf16[64,2048]{1,0:T(8,128)(2,1)}, u32[]{:S(2)}, u32[]{:S(2)}) collective-permute-start(bf16[64,2048]{1,0:T(8,128)(2,1)} %get-tuple-element.637), channel_id=1, source_target_pairs={{0,16},{8,24},{16,0},{24,8},{1,17},{9,25},{17,1},{25,9},{2,18},{10... | collective-permute-start | bytes 786440 | tf_op jit(solution)/shard_map/ppermute | solution.py:27
  1331.2 69.3 %collective-permute-start.200 = (bf16[256,2048]{1,0:T(8,128)(2,1)}, bf16[256,2048]{1,0:T(8,128)(2,1)}, u32[]{:S(2)}, u32[]{:S(2)}) collective-permute-start(bf16[256,2048]{1,0:T(8,128)(2,1)} %slice_bitcast_fusion.6), channel_id=1, source_target_pairs={{0,16},{8,24},{16,0},{24,8},{1,17},{9,25},{17,1},{25,9},{2,18},{10... | collective-permute-start | bytes 3145736 | tf_op jit(solution)/shard_map/ppermute | solution.py:27
  1331.7 66.3 %collective-permute-start.198 = (bf16[256,2048]{1,0:T(8,128)(2,1)}, bf16[256,2048]{1,0:T(8,128)(2,1)}, u32[]{:S(2)}, u32[]{:S(2)}) collective-permute-start(bf16[256,2048]{1,0:T(8,128)(2,1)} %slice_bitcast_fusion.6), channel_id=1, source_target_pairs={{0,8},{8,0},{16,24},{24,16},{1,9},{9,1},{17,25},{25,17},{2,10},{10... | collective-permute-start | bytes 3145736 | tf_op jit(solution)/shard_map/ppermute | solution.py:27
  1333.0 65.2 %collective-permute-start.201 = (bf16[272,2048]{1,0:T(8,128)(2,1)S(1)}, bf16[272,2048]{1,0:T(8,128)(2,1)}, u32[]{:S(2)}, u32[]{:S(2)}) collective-permute-start(bf16[272,2048]{1,0:T(8,128)(2,1)S(1)} %copy-done.74), channel_id=1, source_target_pairs={{0,16},{8,24},{16,0},{24,8},{1,17},{9,25},{17,1},{25,9},{2,18},{10... | collective-permute-start | bytes 3342344 | tf_op jit(solution)/shard_map/ppermute | solution.py:27
  1339.7 62.6 %collective-permute-start.199 = (bf16[272,2048]{1,0:T(8,128)(2,1)S(1)}, bf16[272,2048]{1,0:T(8,128)(2,1)}, u32[]{:S(2)}, u32[]{:S(2)}) collective-permute-start(bf16[272,2048]{1,0:T(8,128)(2,1)S(1)} %copy-done.74), channel_id=1, source_target_pairs={{0,8},{8,0},{16,24},{24,16},{1,9},{9,1},{17,25},{25,17},{2,10},{10... | collective-permute-start | bytes 3342344 | tf_op jit(solution)/shard_map/ppermute | solution.py:27
  (448 other events, 6133.4 us)
Sparse Core Ops, SparseCore 0:
  19.6 66.1 all-gather.14
  87.4 27.6 all-gather.16
  116.6 105.7 all-gather.18
  223.9 58.0 all-gather.20
  283.3 79.4 all-gather.22
  364.8 105.2 all-gather.24
  489.3 57.2 all-gather.26
  775.9 147.1 reduce-scatter.4
  949.9 75.4 reduce-scatter.6
  1116.6 148.6 reduce-scatter.8
  1310.2 77.7 reduce-scatter.10

commit v3 on v2

--- a/solution.py
+++ b/solution.py
@@ -504,6 +504,73 @@
         return list(outs[:-2]), outs[-2], outs[-1]
 
 
+def strip_rows(first, last, start, size):
+    split = first.shape[0]
+    found = []
+    if start < split:
+        count = min(start + size, split) - start
+        found.append((0, first[pl.ds(start, count), :]))
+    if start + size > split:
+        begin = max(start, split)
+        found.append((begin - start, last[pl.ds(begin - split, start + size - begin), :]))
+    return found
+
+
+def place_glu_kernel(count, column_ref, *refs):
+    out_ref, glu_ref = refs[-2:]
+    size = out_ref.shape[1] // count
+    for s in range(count):
+        at = (column_ref[0] ^ s) * size
+        for which in range(3):
+            for offset, rows in strip_rows(refs[2 * s], refs[2 * s + 1], which * size, size):
+                here = pl.ds(pl.multiple_of(at + offset, 16), rows.shape[0])
+                if which == 0:
+                    out_ref[0, here, :] = rows.astype(F32)
+                else:
+                    glu_ref[0, which - 1, here, :] = rows.astype(F32)
+
+
+def place_mix_kernel(count, column_ref, *refs):
+    out_ref, mix_ref, turn_ref = refs[-3:]
+    size = out_ref.shape[1] // count
+    for which in range(4):
+        for s in range(count):
+            at = (column_ref[0] ^ s) * size
+            for offset, rows in strip_rows(refs[2 * s], refs[2 * s + 1], which * size, size):
+                here = pl.ds(pl.multiple_of(at + offset, 16), rows.shape[0])
+                if which == 3:
+                    out_ref[0, here, :] = rows.astype(F32)
+                else:
+                    turn_ref[here, :] = rows.astype(F32)
+        if which < 3:
+            mix_ref[0, which] = turn_ref[...].T
+
+
+def place_strips(body, name, layer, column, slots, kept, shapes, blocks, indices, scratch):
+    flat = [v for halves in slots for v in halves]
+    lanes = blocks[0][-1]
+    kept = list(kept or ())
+    return pl.pallas_call(
+        functools.partial(body, len(slots)),
+        name=name,
+        grid=(flat[0].shape[1] // lanes,),
+        in_specs=[pl.BlockSpec(memory_space=pltpu.SMEM)]
+        + [pl.BlockSpec((v.shape[0], lanes), lambda i: (0, i)) for v in flat]
+        + [pl.BlockSpec(memory_space=pl.ANY) for _ in kept],
+        out_specs=[
+            pl.BlockSpec(block, lambda i, index=index: (layer,) + index(i))
+            for block, index in zip(blocks, indices)
+        ],
+        out_shape=[jax.ShapeDtypeStruct(shape, F32) for shape in shapes],
+        scratch_shapes=scratch,
+        input_output_aliases={1 + len(flat) + k: k for k in range(len(kept))},
+        compiler_params=pltpu.CompilerParams(
+            vmem_limit_bytes=VMEM_LIMIT, dimension_semantics=("arbitrary",)
+        ),
+        cost_estimate=pl.CostEstimate(flops=100, bytes_accessed=1024, transcendentals=0),
+    )(column, *flat, *kept)
+
+
 def matmul(a, b):
     return jnp.dot(a, b, preferred_element_type=F32)
 
@@ -719,17 +786,47 @@
             grads[name] = jnp.zeros((layers,) + value.shape, F32)
         grads[name] = lax.dynamic_update_index_in_dim(grads[name], value.astype(F32), l, 0)
 
+    column_arg = column.astype(jnp.int32).reshape(1)
+    lanes = 512
+    aligned = u_strip % 16 == 0 and width % lanes == 0
+
     def finish_glu(l, slots):
+        if aligned:
+            grads["glus"] = place_strips(
+                place_glu_kernel,
+                "place_glu",
+                l,
+                column_arg,
+                slots,
+                grads.get("glus"),
+                [(layers, units, width), (layers, 2, units, width)],
+                [(1, units, lanes), (1, 2, units, lanes)],
+                [lambda i: (0, i), lambda i: (0, 0, i)],
+                [],
+            )
+            grads["glu_out"] = grads["glus"][0]
+            grads["glu"] = grads["glus"][1].transpose(0, 3, 1, 2)
+            return
         strips = in_columns(slots)
         place("glu_out", l, strips[:, :u_strip].reshape(units, width))
         strips = strips[:, u_strip:].reshape(dp, 2, u_strip, width).transpose(3, 1, 0, 2)
         place("glu", l, strips.reshape(width, 2, units))
 
     def finish_mix(l, slots):
-        strips = in_columns(slots)
-        place("mix_out", l, strips[:, 3 * c_strip :].reshape(channels, width))
-        strips = strips[:, : 3 * c_strip].reshape(dp, 3, c_strip, width).transpose(3, 1, 0, 2)
-        place("mix", l, strips.reshape(width, 3, channels))
+        grads["mixes"] = place_strips(
+            place_mix_kernel,
+            "place_mix",
+            l,
+            column_arg,
+            slots,
+            grads.get("mixes"),
+            [(layers, channels, width), (layers, 3, width, channels)],
+            [(1, channels, lanes), (1, 3, lanes, channels)],
+            [lambda i: (0, i), lambda i: (0, i, 0)],
+            [pltpu.VMEM((channels, lanes), F32)],
+        )
+        grads["mix_out"] = grads["mixes"][0]
+        grads["mix"] = grads["mixes"][1].transpose(0, 2, 1, 3)
 
     for l in reversed(range(layers)):
         (
@@ -795,7 +892,6 @@
             lows.append(jnp.concatenate([low, in_parts(stat)], 1))
         out_grad = gathered(lows)
         if l < layers - 1:
-            out_grad, summed, glu_strips = tie_all(out_grad, summed, glu_strips)
             glu_strips = strips_far(glu_strips)
             mix_strips = strips_far(strips_near(summed))
         padded = jnp.pad(out_w[l], ((0, 0), (0, LANES)))
@@ -817,11 +913,12 @@
             return matmul(rows, mix_w[l])
 
         if l == 0:
-            proj_grad, sent = tie_all(proj_grad, mix_sent(out_part, mix_part))
-            back_first, glu_sum, _ = plane_scatter(*proj_grad[:2], mix_product, glu_sum)
-            back_last, _, (glu_strips, mix_strips) = plane_scatter(
-                *proj_grad[2:], mix_product, (), (glu_strips, mix_strips)
+            sent = mix_sent(out_part, mix_part)
+            proj_grad, sent, glu_sum, glu_strips, mix_strips = tie_all(
+                proj_grad, sent, glu_sum, glu_strips, mix_strips
             )
+            back_first, _, _ = plane_scatter(*proj_grad[:2], mix_product)
+            back_last, _, _ = plane_scatter(*proj_grad[2:], mix_product)
             finish_glu(1, glu_strips)
             finish_mix(1, mix_strips)
         else:
@@ -835,8 +932,11 @@
         )
         mix_gain_parts[l] = sum(gain_part)
         grad = [a + b for a, b in zip(grad, back)]
-        sent, glu_sum = tie_all(sent, glu_sum)
+        if l > 0:
+            sent, glu_sum = tie_all(sent, glu_sum)
         summed = strip_halves(line_scatter(sent))
+        if l == 0:
+            grad, summed = tie_all(grad, summed)
     finish_glu(0, strips_far(strips_near(glu_sum)))
     finish_mix(0, strips_far(strips_near(summed)))
 

time: 1510 us -> 1430 us (0.947)
  other arithmetic: 139 us -> 88 us
  local copies, waits for them, and re-layouts: 232 us -> 192 us
  Pallas kernels: 79.7 us -> 113 us
    pallas_call x0 -> x4, Pallas kernels: none -> 33.4 us  [place_strips(): pl.pallas_call(functools.partial(body, len(slots)), name=name, grid=(flat...]
    another operation x40 -> x16, other arithmetic: 32.1 us -> 4.62 us  [the longest x20 19.1 us: in_columns(): slots = jnp.stack([jnp.concatenate(halves, 0) for halves in slots], 0)]
    unnamed x586 -> x526, local copies, waits for them, and re-layouts: 110 us -> 87.8 us
    dynamic_update_slice x4 -> x0, other arithmetic: 20.9 us -> none  [place(): lax.dynamic_update_index_in_dim(grads[name], value.astype(F32), l, 0)]
  transfers between devices with their start and end apart: 220 -> 220, of which waited for: 108 -> 114; matrix products, arithmetic and copies ran while one was open for 41% -> 38% of each run, Pallas kernels for 5% -> 7%
where the time goes in v3:
time: 1430 us; the launch traced here: 1420 us
  waiting for transfers between devices  472 us (33%)
  matrix products  325 us (23%)
  starting transfers between devices  213 us (15%)
  local copies, waits for them, and re-layouts  192 us (13%)
  Pallas kernels  113 us (8%)
  other arithmetic  88 us (6%)
  between operations  19.1 us (1%)
    ppermute x158, waiting for transfers between devices, swap_dp(): lax.ppermute(v, 'dp', [(i, i ^ bit) for i in range(lax.axis_size('dp'))])  448 us
    ppermute x158, starting transfers between devices, swap_dp(): lax.ppermute(v, 'dp', [(i, i ^ bit) for i in range(lax.axis_size('dp'))])  165 us
    dot_general x40, matrix products, matmul_t(): lax.dot_general(a, b, (((1,), (1,)), ((), ())), preferred_element_type=F32)  134 us
    dot_general x40, matrix products, matmul(): return jnp.dot(a, b, preferred_element_type=F32)  99.4 us
    dot_general x10, matrix products, matmul_rows(): lax.dot_general(a, b, (((0,), (0,)), ((), ())), preferred_element_type=F32)  90.8 us
    unnamed x526, local copies, waits for them, and re-layouts  87.8 us
    pallas_call x8, Pallas kernels, call(): return list(call(self.core, *args))  79.5 us
    pallas_call x4, Pallas kernels, place_strips(): pl.pallas_call(functools.partial(body, len(slots)), name=name, grid=(flat...  33.4 us
  transfers between devices with their start and end apart: 220, of which 114 were waited for; matrix products, arithmetic and copies ran while one was open for 38% of the time, Pallas kernels for 7%

profile of v3, /device:TPU:0, one launch (start us, length us, event | category | flops | bytes accessed | tf_op | source)
XLA Modules:
  0.0 1422.2 jit_solution(2596961055022672891)
XLA Ops:
  21.3 11.2 slice_bitcast_fusion
  65.0 12.3 collective-permute-done.6
  120.8 9.0 mixer_scan.2
  213.5 9.6 collective-permute-done.34
  225.6 9.7 collective-permute-done.23
  361.2 10.6 collective-permute-done.54
  382.8 12.1 collective-permute-done.61
  401.1 10.3 collective-permute-done.64
  639.5 10.5 fusion.19
  653.3 11.2 convolution_convert_fusion.5
  667.1 11.2 convolution_convert_fusion.4
  729.5 11.1 collective-permute-done.109
  793.6 14.6 %mixer_scan_back.2 = (f32[2048,256]{1,0:T(8,128)}, f32[2048,256]{1,0:T(8,128)}, f32[8,256]{1,0:T(8,128)}, f32[8,256]{1,0:T(8,128)}, f32[4,256]{1,0:T(4,128)}, /*index=5*/f32[4,256]{1,0:T(4,128)}) custom-call(s32[1]{0:T(128)} %bitcast.4.core_ref, f32[512,256]{1,0:T(8,128)} %fusion.132.refs_0_, f32[512,256]{1,0:T(8,128)} %fusion.130.refs_1_, ...), custom_call_target="tpu_custom_call" | custom-call | flops 250 | bytes 1024 | tf_op jit(solution)/shard_map/mixer_scan_back/pallas_call | solution.py:424
  817.8 9.3 mixer_project_back.2
  857.5 9.5 convolution_convert_fusion.1
  886.2 10.6 collective-permute-done.143
  899.4 9.7 collective-permute-done.132
  961.1 10.7 fusion.16
  980.4 9.1 convolution_convert_fusion.2
  1023.0 14.0 collective-permute-done.163.refs_3_
  1037.0 9.4 collective-permute-done.160
  1057.0 10.8 collective-permute-done.150
  1080.3 9.7 collective-permute-done.152
  1108.5 13.8 collective-permute-done.166
  1145.8 14.6 %mixer_scan_back.3 = (f32[2048,256]{1,0:T(8,128)}, f32[2048,256]{1,0:T(8,128)}, f32[8,256]{1,0:T(8,128)}, f32[8,256]{1,0:T(8,128)}, f32[4,256]{1,0:T(4,128)}, /*index=5*/f32[4,256]{1,0:T(4,128)}) custom-call(s32[1]{0:T(128)} %bitcast.4.core_ref, f32[512,256]{1,0:T(8,128)} %fusion.124.refs_0_, f32[512,256]{1,0:T(8,128)} %fusion.122.refs_1_, ...), custom_call_target="tpu_custom_call" | custom-call | flops 250 | bytes 1024 | tf_op jit(solution)/shard_map/mixer_scan_back/pallas_call | solution.py:424
  1177.1 9.1 mixer_project_back.3
  1186.2 11.1 convolution_convert_fusion
  1258.7 14.6 %collective-permute-done.198.refs_2_ = bf16[256,2048]{1,0:T(8,128)(2,1)} collective-permute-done((bf16[256,2048]{1,0:T(8,128)(2,1)}, bf16[256,2048]{1,0:T(8,128)(2,1)}, u32[]{:S(2)}, u32[]{:S(2)}) %collective-permute-start.198) | collective-permute-done | bytes 1048608 | tf_op jit(solution)/shard_map/ppermute | solution.py:27
  1316.4 9.7 place_glu.2
  1326.1 18.8 %collective-permute-done.202.refs_6_ = bf16[256,2048]{1,0:T(8,128)(2,1)} collective-permute-done((bf16[256,2048]{1,0:T(8,128)(2,1)}, bf16[256,2048]{1,0:T(8,128)(2,1)}, u32[]{:S(2)}, u32[]{:S(2)}) %collective-permute-start.202) | collective-permute-done | bytes 1048608 | tf_op jit(solution)/shard_map/ppermute | solution.py:27
  1344.9 9.8 place_glu.3
  1380.4 9.7 collective-permute-done.192.refs_2_
  (1337 shorter events, 1045.7 us)
Async XLA Ops:
  7.2 91.7 %all-gather.15.cloned.1.call-start = ((), (), s32[]{:S(2)}) async-start(), calls=%async_computation.8 | async-start | bytes 3932160 | tf_op jit(solution)/shard_map/all_gather | solution.py:160
  19.5 130.5 %all-gather.17.cloned.1.call-start = ((), (), s32[]{:S(2)}) async-start(), calls=%async_computation.9 | async-start | bytes 1310720 | tf_op jit(solution)/shard_map/all_gather | solution.py:160
  38.8 215.2 %all-gather.19.cloned.1.call-start = ((), (), s32[]{:S(2)}) async-start(), calls=%async_computation.10 | async-start | bytes 7208960 | tf_op jit(solution)/shard_map/all_gather | solution.py:160
  62.7 253.6 %all-gather.21.cloned.1.call-start = ((), (), s32[]{:S(2)}) async-start(), calls=%async_computation.11 | async-start | bytes 3604480 | tf_op jit(solution)/shard_map/all_gather | solution.py:160
  165.5 258.9 %all-gather.23.cloned.1.call-start = ((), (), s32[]{:S(2)}) async-start(), calls=%async_computation.12 | async-start | bytes 5242880 | tf_op jit(solution)/shard_map/all_gather | solution.py:160
  247.9 235.1 %all-gather.25.cloned.1.call-start = ((), (), s32[]{:S(2)}) async-start(), calls=%async_computation.13 | async-start | bytes 7208960 | tf_op jit(solution)/shard_map/all_gather | solution.py:160
  334.0 222.3 %all-gather.27.cloned.1.call-start = ((), (), s32[]{:S(2)}) async-start(), calls=%async_computation.14 | async-start | bytes 3604480 | tf_op jit(solution)/shard_map/all_gather | solution.py:160
  477.4 454.9 %reduce-scatter.5.cloned.1.call-start = ((), (), s32[]{:S(2)}) async-start(), calls=%async_computation.4 | async-start | bytes 10813440 | tf_op jit(solution)/shard_map/reduce_scatter | solution.py:164
  619.0 47.4 %collective-permute-start.107 = (bf16[128,2048]{1,0:T(8,128)(2,1)}, bf16[128,2048]{1,0:T(8,128)(2,1)S(1)}, u32[]{:S(2)}, u32[]{:S(2)}) collective-permute-start(bf16[128,2048]{1,0:T(8,128)(2,1)} %pad_maximum_fusion.23), channel_id=1, source_target_pairs={{0,8},{8,0},{16,24},{24,16},{1,9},{9,1},{17,25},{25,17},{2,10},{10... | collective-permute-start | bytes 1572872 | tf_op jit(solution)/shard_map/ppermute | solution.py:27
  621.6 45.5 %collective-permute-start.108 = (bf16[128,2048]{1,0:T(8,128)(2,1)}, bf16[128,2048]{1,0:T(8,128)(2,1)}, u32[]{:S(2)}, u32[]{:S(2)}) collective-permute-start(bf16[128,2048]{1,0:T(8,128)(2,1)} %pad_maximum_fusion.24), channel_id=1, source_target_pairs={{0,16},{8,24},{16,0},{24,8},{1,17},{9,25},{17,1},{25,9},{2,18},{10... | collective-permute-start | bytes 1572872 | tf_op jit(solution)/shard_map/ppermute | solution.py:27
  624.3 42.8 %collective-permute-start.87 = (bf16[128,2048]{1,0:T(8,128)(2,1)}, bf16[128,2048]{1,0:T(8,128)(2,1)}, u32[]{:S(2)}, u32[]{:S(2)}) collective-permute-start(bf16[128,2048]{1,0:T(8,128)(2,1)} %pad_maximum_fusion.17), channel_id=1, source_target_pairs={{0,8},{8,0},{16,24},{24,16},{1,9},{9,1},{17,25},{25,17},{2,10},{10... | collective-permute-start | bytes 1572872 | tf_op jit(solution)/shard_map/ppermute | solution.py:27
  627.2 39.9 %collective-permute-start.88 = (bf16[128,2048]{1,0:T(8,128)(2,1)}, bf16[128,2048]{1,0:T(8,128)(2,1)}, u32[]{:S(2)}, u32[]{:S(2)}) collective-permute-start(bf16[128,2048]{1,0:T(8,128)(2,1)} %pad_maximum_fusion.18), channel_id=1, source_target_pairs={{0,16},{8,24},{16,0},{24,8},{1,17},{9,25},{17,1},{25,9},{2,18},{10... | collective-permute-start | bytes 1572872 | tf_op jit(solution)/shard_map/ppermute | solution.py:27
  639.5 38.9 %collective-permute-start.114 = (bf16[512,2048]{1,0:T(8,128)(2,1)}, bf16[512,2048]{1,0:T(8,128)(2,1)S(1)}, u32[]{:S(2)}, u32[]{:S(2)}) collective-permute-start(bf16[512,2048]{1,0:T(8,128)(2,1)} %add_convert_fusion.2), channel_id=1, source_target_pairs={{0,1},{1,0},{2,3},{3,2},{4,5},{5,4},{6,7},{7,6},{8,9},{9,8},{10,11... | collective-permute-start | bytes 6291464 | tf_op jit(solution)/shard_map/ppermute | solution.py:31
  767.0 283.2 %reduce-scatter.7.cloned.1.call-start = ((), (), s32[]{:S(2)}) async-start(), calls=%async_computation.5 | async-start | bytes 5242880 | tf_op jit(solution)/shard_map/reduce_scatter | solution.py:164
  937.0 68.4 %collective-permute-start.164 = (bf16[256,2048]{1,0:T(8,128)(2,1)}, bf16[256,2048]{1,0:T(8,128)(2,1)}, u32[]{:S(2)}, u32[]{:S(2)}) collective-permute-start(bf16[256,2048]{1,0:T(8,128)(2,1)} %slice_bitcast_fusion.7.refs_0_), channel_id=1, source_target_pairs={{0,16},{8,24},{16,0},{24,8},{1,17},{9,25},{17,1},{25,9},{2,18},{10... | collective-permute-start | bytes 3145736 | tf_op jit(solution)/shard_map/ppermute | solution.py:27
  938.0 84.9 %collective-permute-start.162 = (bf16[256,2048]{1,0:T(8,128)(2,1)}, bf16[256,2048]{1,0:T(8,128)(2,1)}, u32[]{:S(2)}, u32[]{:S(2)}) collective-permute-start(bf16[256,2048]{1,0:T(8,128)(2,1)} %slice_bitcast_fusion.7.refs_0_), channel_id=1, source_target_pairs={{0,8},{8,0},{16,24},{24,16},{1,9},{9,1},{17,25},{25,17},{2,10},{10... | collective-permute-start | bytes 3145736 | tf_op jit(solution)/shard_map/ppermute | solution.py:27
  939.4 264.4 %reduce-scatter.9.cloned.1.call-start = ((), (), s32[]{:S(2)}) async-start(), calls=%async_computation.6 | async-start | bytes 10813440 | tf_op jit(solution)/shard_map/reduce_scatter | solution.py:164
  939.7 83.3 %collective-permute-start.165 = (bf16[272,2048]{1,0:T(8,128)(2,1)}, bf16[272,2048]{1,0:T(8,128)(2,1)}, u32[]{:S(2)}, u32[]{:S(2)}) collective-permute-start(bf16[272,2048]{1,0:T(8,128)(2,1)} %slice_bitcast_fusion.5.refs_1_), channel_id=1, source_target_pairs={{0,16},{8,24},{16,0},{24,8},{1,17},{9,25},{17,1},{25,9},{2,18},{10... | collective-permute-start | bytes 3342344 | tf_op jit(solution)/shard_map/ppermute | solution.py:27
  951.7 44.2 %collective-permute-start.147 = (bf16[512,2048]{1,0:T(8,128)(2,1)}, bf16[512,2048]{1,0:T(8,128)(2,1)S(1)}, u32[]{:S(2)}, u32[]{:S(2)}) collective-permute-start(bf16[512,2048]{1,0:T(8,128)(2,1)} %add_convert_fusion.1), channel_id=1, source_target_pairs={{0,1},{1,0},{2,3},{3,2},{4,5},{5,4},{6,7},{7,6},{8,9},{9,8},{10,11... | collective-permute-start | bytes 6291464 | tf_op jit(solution)/shard_map/ppermute | solution.py:31
  1013.2 33.3 %collective-permute-start.160 = (bf16[128,2048]{1,0:T(8,128)(2,1)S(1)}, bf16[128,2048]{1,0:T(8,128)(2,1)S(1)}, u32[]{:S(2)}, u32[]{:S(2)}) collective-permute-start(bf16[128,2048]{1,0:T(8,128)(2,1)S(1)} %pad_maximum_fusion.33), channel_id=1, source_target_pairs={{0,8},{8,0},{16,24},{24,16},{1,9},{9,1},{17,25},{25,17},{2,10},{10... | collective-permute-start | bytes 1572872 | tf_op jit(solution)/shard_map/ppermute | solution.py:27
  1052.6 321.1 %reduce-scatter.11.cloned.1.call-start = ((), (), s32[]{:S(2)}) async-start(), calls=%async_computation.7 | async-start | bytes 5242880 | tf_op jit(solution)/shard_map/reduce_scatter | solution.py:164
  1135.9 65.0 %collective-permute-start.174 = (bf16[256,2048]{1,0:T(8,128)(2,1)}, bf16[256,2048]{1,0:T(8,128)(2,1)}, u32[]{:S(2)}, u32[]{:S(2)}) collective-permute-start(bf16[256,2048]{1,0:T(8,128)(2,1)} %collective-permute-done.162.refs_2_), channel_id=1, source_target_pairs={{0,16},{8,24},{16,0},{24,8},{1,17},{9,25},{17,1},{25,9},{2,18},{10... | collective-permute-start | bytes 3145736 | tf_op jit(solution)/shard_map/ppermute | solution.py:27
  1137.1 71.6 %collective-permute-start.175 = (bf16[272,2048]{1,0:T(8,128)(2,1)}, bf16[272,2048]{1,0:T(8,128)(2,1)}, u32[]{:S(2)}, u32[]{:S(2)}) collective-permute-start(bf16[272,2048]{1,0:T(8,128)(2,1)} %collective-permute-done.165.refs_5_), channel_id=1, source_target_pairs={{0,8},{8,0},{16,24},{24,16},{1,9},{9,1},{17,25},{25,17},{2,10},{10... | collective-permute-start | bytes 3342344 | tf_op jit(solution)/shard_map/ppermute | solution.py:27
  1173.0 35.6 %collective-permute-start.178 = (bf16[128,2048]{1,0:T(8,128)(2,1)}, bf16[128,2048]{1,0:T(8,128)(2,1)}, u32[]{:S(2)}, u32[]{:S(2)}) collective-permute-start(bf16[128,2048]{1,0:T(8,128)(2,1)} %get-tuple-element.392.refs_0_), channel_id=1, source_target_pairs={{0,16},{8,24},{16,0},{24,8},{1,17},{9,25},{17,1},{25,9},{2,18},{10... | collective-permute-start | bytes 1572872 | tf_op jit(solution)/shard_map/ppermute | solution.py:27
  1245.1 33.2 %collective-permute-start.201 = (bf16[272,2048]{1,0:T(8,128)(2,1)}, bf16[272,2048]{1,0:T(8,128)(2,1)}, u32[]{:S(2)}, u32[]{:S(2)}) collective-permute-start(bf16[272,2048]{1,0:T(8,128)(2,1)} %slice_bitcast_fusion.4.refs_1_), channel_id=1, source_target_pairs={{0,16},{8,24},{16,0},{24,8},{1,17},{9,25},{17,1},{25,9},{2,18},{10... | collective-permute-start | bytes 3342344 | tf_op jit(solution)/shard_map/ppermute | solution.py:27
  1255.4 34.1 %collective-permute-start.186 = (bf16[128,2048]{1,0:T(8,128)(2,1)S(1)}, bf16[128,2048]{1,0:T(8,128)(2,1)}, u32[]{:S(2)}, u32[]{:S(2)}) collective-permute-start(bf16[128,2048]{1,0:T(8,128)(2,1)S(1)} %pad_maximum_fusion.36), channel_id=1, source_target_pairs={{0,16},{8,24},{16,0},{24,8},{1,17},{9,25},{17,1},{25,9},{2,18},{10... | collective-permute-start | bytes 1572872 | tf_op jit(solution)/shard_map/ppermute | solution.py:27
  1256.6 39.1 %collective-permute-start.190 = (bf16[128,2048]{1,0:T(8,128)(2,1)S(1)}, bf16[128,2048]{1,0:T(8,128)(2,1)}, u32[]{:S(2)}, u32[]{:S(2)}) collective-permute-start(bf16[128,2048]{1,0:T(8,128)(2,1)S(1)} %pad_maximum_fusion.37), channel_id=1, source_target_pairs={{0,8},{8,0},{16,24},{24,16},{1,9},{9,1},{17,25},{25,17},{2,10},{10... | collective-permute-start | bytes 1572872 | tf_op jit(solution)/shard_map/ppermute | solution.py:27
  1278.3 47.8 %collective-permute-start.199 = (bf16[272,2048]{1,0:T(8,128)(2,1)}, bf16[272,2048]{1,0:T(8,128)(2,1)}, u32[]{:S(2)}, u32[]{:S(2)}) collective-permute-start(bf16[272,2048]{1,0:T(8,128)(2,1)} %slice_bitcast_fusion.4.refs_1_), channel_id=1, source_target_pairs={{0,8},{8,0},{16,24},{24,16},{1,9},{9,1},{17,25},{25,17},{2,10},{10... | collective-permute-start | bytes 3342344 | tf_op jit(solution)/shard_map/ppermute | solution.py:27
  1284.5 60.4 %collective-permute-start.203 = (bf16[272,2048]{1,0:T(8,128)(2,1)}, bf16[272,2048]{1,0:T(8,128)(2,1)}, u32[]{:S(2)}, u32[]{:S(2)}) collective-permute-start(bf16[272,2048]{1,0:T(8,128)(2,1)} %collective-permute-done.201.refs_5_), channel_id=1, source_target_pairs={{0,8},{8,0},{16,24},{24,16},{1,9},{9,1},{17,25},{25,17},{2,10},{10... | collective-permute-start | bytes 3342344 | tf_op jit(solution)/shard_map/ppermute | solution.py:27
  1289.5 36.5 %collective-permute-start.200 = (bf16[256,2048]{1,0:T(8,128)(2,1)}, bf16[256,2048]{1,0:T(8,128)(2,1)}, u32[]{:S(2)}, u32[]{:S(2)}) collective-permute-start(bf16[256,2048]{1,0:T(8,128)(2,1)} %slice_bitcast_fusion.6.refs_0_), channel_id=1, source_target_pairs={{0,16},{8,24},{16,0},{24,8},{1,17},{9,25},{17,1},{25,9},{2,18},{10... | collective-permute-start | bytes 3145736 | tf_op jit(solution)/shard_map/ppermute | solution.py:27
  1295.7 49.2 %collective-permute-start.202 = (bf16[256,2048]{1,0:T(8,128)(2,1)}, bf16[256,2048]{1,0:T(8,128)(2,1)}, u32[]{:S(2)}, u32[]{:S(2)}) collective-permute-start(bf16[256,2048]{1,0:T(8,128)(2,1)} %collective-permute-done.198.refs_2_), channel_id=1, source_target_pairs={{0,16},{8,24},{16,0},{24,8},{1,17},{9,25},{17,1},{25,9},{2,18},{10... | collective-permute-start | bytes 3145736 | tf_op jit(solution)/shard_map/ppermute | solution.py:27
  1305.5 49.3 %collective-permute-start.205 = (f32[8,2048]{1,0:T(8,128)S(1)}, f32[8,2048]{1,0:T(8,128)S(1)}, u32[]{:S(2)}, u32[]{:S(2)}) collective-permute-start(f32[8,2048]{1,0:T(8,128)S(1)} %add.798), channel_id=1, source_target_pairs={{0,8},{8,0},{16,24},{24,16},{1,9},{9,1},{17,25},{25,17},{2,10},{10... | collective-permute-start | bytes 196616 | tf_op jit(solution)/shard_map/ppermute | solution.py:27
  (416 other events, 5999.9 us)
Sparse Core Ops, SparseCore 0:
  19.6 66.1 all-gather.14
  87.4 27.5 all-gather.16
  116.6 105.8 all-gather.18
  223.9 58.0 all-gather.20
  283.3 79.4 all-gather.22
  364.8 105.2 all-gather.24
  477.5 59.5 all-gather.26
  767.1 149.4 reduce-scatter.4
  939.6 77.9 reduce-scatter.6
  1052.7 149.7 reduce-scatter.8
  1227.9 79.3 reduce-scatter.10

commit v4 on v3

--- a/solution.py
+++ b/solution.py
@@ -139,12 +139,13 @@
 
 
 def sum_all(v):
+    v = line_sum(v)
     v = v + swap_core(v)
     bit = 1
     while bit < lax.axis_size("dp"):
         v = v + swap_dp(v, bit)
         bit *= 2
-    return line_sum(v)
+    return v
 
 
 def tie_all(*values):
@@ -743,7 +744,7 @@
 
         def glu(rows):
             a, b = matmul_t(rows, gate_w[l]), matmul_t(rows, up_w[l])
-            return a, b, (jax.nn.silu(a) * b).astype(BF16)
+            return a.astype(BF16), b.astype(BF16), (jax.nn.silu(a) * b).astype(BF16)
 
         if l == 0:
             glu_in, grad_low = tie_all(glu_in, [rows.astype(BF16) for rows in grad])
@@ -853,6 +854,7 @@
 
         def glu_back(rows, a, b):
             dhidden = matmul_t(rows, down_w[l])
+            a, b = a.astype(F32), b.astype(F32)
             sig = jax.nn.sigmoid(a)
             dgate = (dhidden * b * sig * (1.0 + a * (1.0 - sig))).astype(BF16)
             return Pair(dgate, (dhidden * a * sig).astype(BF16))
@@ -914,13 +916,14 @@
 
         if l == 0:
             sent = mix_sent(out_part, mix_part)
-            proj_grad, sent, glu_sum, glu_strips, mix_strips = tie_all(
-                proj_grad, sent, glu_sum, glu_strips, mix_strips
-            )
+            proj_grad, sent, glu_sum = tie_all(proj_grad, sent, glu_sum)
+            proj_grad, glu_strips, mix_strips = tie_all(proj_grad, glu_strips, mix_strips)
             back_first, _, _ = plane_scatter(*proj_grad[:2], mix_product)
-            back_last, _, _ = plane_scatter(*proj_grad[2:], mix_product)
             finish_glu(1, glu_strips)
             finish_mix(1, mix_strips)
+            fill = {name: grads[name] for name in ("glus", "mixes") if name in grads}
+            back_last, _, fill = plane_scatter(*proj_grad[2:], mix_product, (), fill)
+            grads.update(fill)
         else:
             back_first, _, _ = plane_scatter(*proj_grad[:2], mix_product)
             back_last, out_part, mix_part = plane_scatter(
@@ -938,7 +941,7 @@
         if l == 0:
             grad, summed = tie_all(grad, summed)
     finish_glu(0, strips_far(strips_near(glu_sum)))
-    finish_mix(0, strips_far(strips_near(summed)))
+    mix_strips = strips_near(summed)
 
     def spread(row):
         zeros = jnp.zeros((line, 2, dp, c_strip), F32)
@@ -952,6 +955,8 @@
         + [spread(v) for v in out_gain_parts]
         + [spread(v) for v in bound_parts]
     )
+    rows, mix_strips = tie_all(rows, mix_strips)
+    finish_mix(0, strips_far(mix_strips))
     rows = sum_all(rows)
     mix_gain_grad = rows[:layers]
     glu_gain_grad = rows[layers : 2 * layers]

time: 1430 us -> 1430 us (level)
    ppermute x158, waiting for transfers between devices: 448 us -> 417 us  [swap_dp(): lax.ppermute(v, 'dp', [(i, i ^ bit) for i in range(lax.axis_size('dp'))])]
    reduce_scatter x4, waiting for transfers between devices: 0.03 us -> 18.3 us  [line_scatter(): lax.psum_scatter(v, 'mp', scatter_dimension=0, tiled=True, axis_index_gro...]
    unnamed x526 -> x534, local copies, waits for them, and re-layouts: 87.8 us -> 87.1 us
  transfers between devices with their start and end apart: 220 -> 220, of which waited for: 114 -> 112; matrix products, arithmetic and copies ran while one was open for 38% -> 39% of each run, Pallas kernels for 7% -> 8%
where the time goes in v4:
time: 1430 us; the launch traced here: 1420 us
  waiting for transfers between devices  463 us (32%)
  matrix products  328 us (23%)
  starting transfers between devices  217 us (15%)
  local copies, waits for them, and re-layouts  192 us (13%)
  Pallas kernels  114 us (8%)
  other arithmetic  89.9 us (6%)
  between operations  19.2 us (1%)
    ppermute x158, waiting for transfers between devices, swap_dp(): lax.ppermute(v, 'dp', [(i, i ^ bit) for i in range(lax.axis_size('dp'))])  417 us
    ppermute x158, starting transfers between devices, swap_dp(): lax.ppermute(v, 'dp', [(i, i ^ bit) for i in range(lax.axis_size('dp'))])  171 us
    dot_general x40, matrix products, matmul_t(): lax.dot_general(a, b, (((1,), (1,)), ((), ())), preferred_element_type=F32)  134 us
    dot_general x40, matrix products, matmul(): return jnp.dot(a, b, preferred_element_type=F32)  99.3 us
    dot_general x10, matrix products, matmul_rows(): lax.dot_general(a, b, (((0,), (0,)), ((), ())), preferred_element_type=F32)  94.3 us
    unnamed x534, local copies, waits for them, and re-layouts  87.1 us
    pallas_call x8, Pallas kernels, call(): return list(call(self.core, *args))  79.5 us
    pallas_call x4, Pallas kernels, place_strips(): pl.pallas_call(functools.partial(body, len(slots)), name=name, grid=(flat...  34.4 us
  transfers between devices with their start and end apart: 220, of which 112 were waited for; matrix products, arithmetic and copies ran while one was open for 39% of the time, Pallas kernels for 8%

profile of v4, /device:TPU:0, one launch (start us, length us, event | category | flops | bytes accessed | tf_op | source)
XLA Modules:
  0.0 1422.9 jit_solution(7697447551463863875)
XLA Ops:
  21.3 11.2 slice_bitcast_fusion
  65.1 12.3 collective-permute-done.6
  120.8 9.0 mixer_scan.2
  213.8 9.6 collective-permute-done.34
  225.8 9.6 collective-permute-done.23
  360.5 10.6 collective-permute-done.54
  382.2 12.1 collective-permute-done.61
  400.4 10.4 collective-permute-done.64
  640.1 10.4 fusion.19
  653.9 11.2 convolution_convert_fusion.5
  667.7 11.2 convolution_convert_fusion.4
  729.8 11.6 collective-permute-done.109
  794.4 14.6 %mixer_scan_back.2 = (f32[2048,256]{1,0:T(8,128)}, f32[2048,256]{1,0:T(8,128)}, f32[8,256]{1,0:T(8,128)}, f32[8,256]{1,0:T(8,128)}, f32[4,256]{1,0:T(4,128)}, /*index=5*/f32[4,256]{1,0:T(4,128)}) custom-call(s32[1]{0:T(128)} %bitcast.4.core_ref, f32[512,256]{1,0:T(8,128)} %fusion.196.refs_0_, f32[512,256]{1,0:T(8,128)} %fusion.194.refs_1_, ...), custom_call_target="tpu_custom_call" | custom-call | flops 250 | bytes 1024 | tf_op jit(solution)/shard_map/mixer_scan_back/pallas_call | solution.py:425
  818.6 9.3 mixer_project_back.2
  858.2 9.5 convolution_convert_fusion.1
  887.6 10.6 collective-permute-done.143
  900.3 9.4 collective-permute-done.132
  961.7 10.7 fusion.16
  980.7 9.1 convolution_convert_fusion.2
  1024.2 13.0 collective-permute-done.163.refs_3_
  1037.2 9.4 collective-permute-done.160
  1058.1 9.9 collective-permute-done.150
  1080.6 11.0 collective-permute-done.152
  1109.5 12.8 collective-permute-done.166
  1146.9 14.6 %mixer_scan_back.3 = (f32[2048,256]{1,0:T(8,128)}, f32[2048,256]{1,0:T(8,128)}, f32[8,256]{1,0:T(8,128)}, f32[8,256]{1,0:T(8,128)}, f32[4,256]{1,0:T(4,128)}, /*index=5*/f32[4,256]{1,0:T(4,128)}) custom-call(s32[1]{0:T(128)} %bitcast.4.core_ref, f32[512,256]{1,0:T(8,128)} %fusion.188.refs_0_, f32[512,256]{1,0:T(8,128)} %fusion.186.refs_1_, ...), custom_call_target="tpu_custom_call" | custom-call | flops 250 | bytes 1024 | tf_op jit(solution)/shard_map/mixer_scan_back/pallas_call | solution.py:425
  1177.5 9.1 mixer_project_back.3
  1186.6 11.1 convolution_convert_fusion
  1269.8 11.2 place_glu.2
  1288.9 18.3 %reduce-scatter.11.cloned.1.call-done = bf16[1,256,2048]{2,1,0:T(8,128)(2,1)} async-done(((bf16[4,256,2048]{2,1,0:T(8,128)(2,1)}), bf16[1,256,2048]{2,1,0:T(8,128)(2,1)}) %reduce-scatter.11.cloned.1.call-update) | async-done | bytes 1048592 | tf_op jit(solution)/shard_map/reduce_scatter | solution.py:165
  1314.1 9.3 collective-permute-done.194.refs_4_
  1360.1 18.4 %collective-permute-done.202.refs_6_ = bf16[256,2048]{1,0:T(8,128)(2,1)} collective-permute-done((bf16[256,2048]{1,0:T(8,128)(2,1)}, bf16[256,2048]{1,0:T(8,128)(2,1)}, u32[]{:S(2)}, u32[]{:S(2)}) %collective-permute-start.202) | collective-permute-done | bytes 1048608 | tf_op jit(solution)/shard_map/ppermute | solution.py:27
  1383.3 9.7 place_glu.3
  (1344 shorter events, 1043.4 us)
Async XLA Ops:
  7.2 91.8 %all-gather.15.cloned.1.call-start = ((), (), s32[]{:S(2)}) async-start(), calls=%async_computation.8 | async-start | bytes 3932160 | tf_op jit(solution)/shard_map/all_gather | solution.py:161
  19.5 130.5 %all-gather.17.cloned.1.call-start = ((), (), s32[]{:S(2)}) async-start(), calls=%async_computation.9 | async-start | bytes 1310720 | tf_op jit(solution)/shard_map/all_gather | solution.py:161
  38.8 215.1 %all-gather.19.cloned.1.call-start = ((), (), s32[]{:S(2)}) async-start(), calls=%async_computation.10 | async-start | bytes 7208960 | tf_op jit(solution)/shard_map/all_gather | solution.py:161
  62.7 252.9 %all-gather.21.cloned.1.call-start = ((), (), s32[]{:S(2)}) async-start(), calls=%async_computation.11 | async-start | bytes 3604480 | tf_op jit(solution)/shard_map/all_gather | solution.py:161
  165.7 258.0 %all-gather.23.cloned.1.call-start = ((), (), s32[]{:S(2)}) async-start(), calls=%async_computation.12 | async-start | bytes 5242880 | tf_op jit(solution)/shard_map/all_gather | solution.py:161
  248.1 234.0 %all-gather.25.cloned.1.call-start = ((), (), s32[]{:S(2)}) async-start(), calls=%async_computation.13 | async-start | bytes 7208960 | tf_op jit(solution)/shard_map/all_gather | solution.py:161
  333.3 222.2 %all-gather.27.cloned.1.call-start = ((), (), s32[]{:S(2)}) async-start(), calls=%async_computation.14 | async-start | bytes 3604480 | tf_op jit(solution)/shard_map/all_gather | solution.py:161
  476.5 457.3 %reduce-scatter.5.cloned.1.call-start = ((), (), s32[]{:S(2)}) async-start(), calls=%async_computation.4 | async-start | bytes 10813440 | tf_op jit(solution)/shard_map/reduce_scatter | solution.py:165
  619.3 47.8 %collective-permute-start.107 = (bf16[128,2048]{1,0:T(8,128)(2,1)}, bf16[128,2048]{1,0:T(8,128)(2,1)S(1)}, u32[]{:S(2)}, u32[]{:S(2)}) collective-permute-start(bf16[128,2048]{1,0:T(8,128)(2,1)} %pad_maximum_fusion.23), channel_id=1, source_target_pairs={{0,8},{8,0},{16,24},{24,16},{1,9},{9,1},{17,25},{25,17},{2,10},{10... | collective-permute-start | bytes 1572872 | tf_op jit(solution)/shard_map/ppermute | solution.py:27
  621.6 46.0 %collective-permute-start.108 = (bf16[128,2048]{1,0:T(8,128)(2,1)}, bf16[128,2048]{1,0:T(8,128)(2,1)}, u32[]{:S(2)}, u32[]{:S(2)}) collective-permute-start(bf16[128,2048]{1,0:T(8,128)(2,1)} %pad_maximum_fusion.24), channel_id=1, source_target_pairs={{0,16},{8,24},{16,0},{24,8},{1,17},{9,25},{17,1},{25,9},{2,18},{10... | collective-permute-start | bytes 1572872 | tf_op jit(solution)/shard_map/ppermute | solution.py:27
  624.5 43.1 %collective-permute-start.87 = (bf16[128,2048]{1,0:T(8,128)(2,1)}, bf16[128,2048]{1,0:T(8,128)(2,1)}, u32[]{:S(2)}, u32[]{:S(2)}) collective-permute-start(bf16[128,2048]{1,0:T(8,128)(2,1)} %pad_maximum_fusion.17), channel_id=1, source_target_pairs={{0,8},{8,0},{16,24},{24,16},{1,9},{9,1},{17,25},{25,17},{2,10},{10... | collective-permute-start | bytes 1572872 | tf_op jit(solution)/shard_map/ppermute | solution.py:27
  627.3 40.3 %collective-permute-start.88 = (bf16[128,2048]{1,0:T(8,128)(2,1)}, bf16[128,2048]{1,0:T(8,128)(2,1)}, u32[]{:S(2)}, u32[]{:S(2)}) collective-permute-start(bf16[128,2048]{1,0:T(8,128)(2,1)} %pad_maximum_fusion.18), channel_id=1, source_target_pairs={{0,16},{8,24},{16,0},{24,8},{1,17},{9,25},{17,1},{25,9},{2,18},{10... | collective-permute-start | bytes 1572872 | tf_op jit(solution)/shard_map/ppermute | solution.py:27
  640.1 38.9 %collective-permute-start.114 = (bf16[512,2048]{1,0:T(8,128)(2,1)}, bf16[512,2048]{1,0:T(8,128)(2,1)S(1)}, u32[]{:S(2)}, u32[]{:S(2)}) collective-permute-start(bf16[512,2048]{1,0:T(8,128)(2,1)} %add_convert_fusion.2), channel_id=1, source_target_pairs={{0,1},{1,0},{2,3},{3,2},{4,5},{5,4},{6,7},{7,6},{8,9},{9,8},{10,11... | collective-permute-start | bytes 6291464 | tf_op jit(solution)/shard_map/ppermute | solution.py:31
  767.3 283.1 %reduce-scatter.7.cloned.1.call-start = ((), (), s32[]{:S(2)}) async-start(), calls=%async_computation.5 | async-start | bytes 5242880 | tf_op jit(solution)/shard_map/reduce_scatter | solution.py:165
  938.6 68.0 %collective-permute-start.164 = (bf16[256,2048]{1,0:T(8,128)(2,1)}, bf16[256,2048]{1,0:T(8,128)(2,1)}, u32[]{:S(2)}, u32[]{:S(2)}) collective-permute-start(bf16[256,2048]{1,0:T(8,128)(2,1)} %slice_bitcast_fusion.7.refs_0_), channel_id=1, source_target_pairs={{0,16},{8,24},{16,0},{24,8},{1,17},{9,25},{17,1},{25,9},{2,18},{10... | collective-permute-start | bytes 3145736 | tf_op jit(solution)/shard_map/ppermute | solution.py:27
  939.6 84.6 %collective-permute-start.162 = (bf16[256,2048]{1,0:T(8,128)(2,1)}, bf16[256,2048]{1,0:T(8,128)(2,1)}, u32[]{:S(2)}, u32[]{:S(2)}) collective-permute-start(bf16[256,2048]{1,0:T(8,128)(2,1)} %slice_bitcast_fusion.7.refs_0_), channel_id=1, source_target_pairs={{0,8},{8,0},{16,24},{24,16},{1,9},{9,1},{17,25},{25,17},{2,10},{10... | collective-permute-start | bytes 3145736 | tf_op jit(solution)/shard_map/ppermute | solution.py:27
  940.1 264.1 %reduce-scatter.9.cloned.1.call-start = ((), (), s32[]{:S(2)}) async-start(), calls=%async_computation.6 | async-start | bytes 10813440 | tf_op jit(solution)/shard_map/reduce_scatter | solution.py:165
  940.4 83.8 %collective-permute-start.165 = (bf16[272,2048]{1,0:T(8,128)(2,1)}, bf16[272,2048]{1,0:T(8,128)(2,1)}, u32[]{:S(2)}, u32[]{:S(2)}) collective-permute-start(bf16[272,2048]{1,0:T(8,128)(2,1)} %slice_bitcast_fusion.5.refs_1_), channel_id=1, source_target_pairs={{0,16},{8,24},{16,0},{24,8},{1,17},{9,25},{17,1},{25,9},{2,18},{10... | collective-permute-start | bytes 3342344 | tf_op jit(solution)/shard_map/ppermute | solution.py:27
  952.2 45.2 %collective-permute-start.147 = (bf16[512,2048]{1,0:T(8,128)(2,1)}, bf16[512,2048]{1,0:T(8,128)(2,1)S(1)}, u32[]{:S(2)}, u32[]{:S(2)}) collective-permute-start(bf16[512,2048]{1,0:T(8,128)(2,1)} %add_convert_fusion.1), channel_id=1, source_target_pairs={{0,1},{1,0},{2,3},{3,2},{4,5},{5,4},{6,7},{7,6},{8,9},{9,8},{10,11... | collective-permute-start | bytes 6291464 | tf_op jit(solution)/shard_map/ppermute | solution.py:31
  961.2 32.4 %collective-permute-start.157 = (bf16[512,2048]{1,0:T(8,128)(2,1)}, bf16[512,2048]{1,0:T(8,128)(2,1)S(1)}, u32[]{:S(2)}, u32[]{:S(2)}) collective-permute-start(bf16[512,2048]{1,0:T(8,128)(2,1)} %add_convert_fusion), channel_id=1, source_target_pairs={{0,1},{1,0},{2,3},{3,2},{4,5},{5,4},{6,7},{7,6},{8,9},{9,8},{10,11... | collective-permute-start | bytes 6291464 | tf_op jit(solution)/shard_map/ppermute | solution.py:31
  1013.4 33.3 %collective-permute-start.160 = (bf16[128,2048]{1,0:T(8,128)(2,1)S(1)}, bf16[128,2048]{1,0:T(8,128)(2,1)S(1)}, u32[]{:S(2)}, u32[]{:S(2)}) collective-permute-start(bf16[128,2048]{1,0:T(8,128)(2,1)S(1)} %pad_maximum_fusion.33), channel_id=1, source_target_pairs={{0,8},{8,0},{16,24},{24,16},{1,9},{9,1},{17,25},{25,17},{2,10},{10... | collective-permute-start | bytes 1572872 | tf_op jit(solution)/shard_map/ppermute | solution.py:27
  1014.9 31.8 %collective-permute-start.161 = (bf16[128,2048]{1,0:T(8,128)(2,1)S(1)}, bf16[128,2048]{1,0:T(8,128)(2,1)S(1)}, u32[]{:S(2)}, u32[]{:S(2)}) collective-permute-start(bf16[128,2048]{1,0:T(8,128)(2,1)S(1)} %pad_maximum_fusion.34), channel_id=1, source_target_pairs={{0,16},{8,24},{16,0},{24,8},{1,17},{9,25},{17,1},{25,9},{2,18},{10... | collective-permute-start | bytes 1572872 | tf_op jit(solution)/shard_map/ppermute | solution.py:27
  1052.7 254.5 %reduce-scatter.11.cloned.1.call-start = ((), (), s32[]{:S(2)}) async-start(), calls=%async_computation.7 | async-start | bytes 5242880 | tf_op jit(solution)/shard_map/reduce_scatter | solution.py:165
  1136.4 64.9 %collective-permute-start.174 = (bf16[256,2048]{1,0:T(8,128)(2,1)}, bf16[256,2048]{1,0:T(8,128)(2,1)}, u32[]{:S(2)}, u32[]{:S(2)}) collective-permute-start(bf16[256,2048]{1,0:T(8,128)(2,1)} %collective-permute-done.162.refs_2_), channel_id=1, source_target_pairs={{0,16},{8,24},{16,0},{24,8},{1,17},{9,25},{17,1},{25,9},{2,18},{10... | collective-permute-start | bytes 3145736 | tf_op jit(solution)/shard_map/ppermute | solution.py:27
  1137.4 71.6 %collective-permute-start.175 = (bf16[272,2048]{1,0:T(8,128)(2,1)}, bf16[272,2048]{1,0:T(8,128)(2,1)}, u32[]{:S(2)}, u32[]{:S(2)}) collective-permute-start(bf16[272,2048]{1,0:T(8,128)(2,1)} %collective-permute-done.165.refs_5_), channel_id=1, source_target_pairs={{0,8},{8,0},{16,24},{24,16},{1,9},{9,1},{17,25},{25,17},{2,10},{10... | collective-permute-start | bytes 3342344 | tf_op jit(solution)/shard_map/ppermute | solution.py:27
  1174.1 34.9 %collective-permute-start.178 = (bf16[128,2048]{1,0:T(8,128)(2,1)}, bf16[128,2048]{1,0:T(8,128)(2,1)}, u32[]{:S(2)}, u32[]{:S(2)}) collective-permute-start(bf16[128,2048]{1,0:T(8,128)(2,1)} %get-tuple-element.414.refs_0_), channel_id=1, source_target_pairs={{0,16},{8,24},{16,0},{24,8},{1,17},{9,25},{17,1},{25,9},{2,18},{10... | collective-permute-start | bytes 1572872 | tf_op jit(solution)/shard_map/ppermute | solution.py:27
  1261.5 50.6 %collective-permute-start.198 = (bf16[256,2048]{1,0:T(8,128)(2,1)}, bf16[256,2048]{1,0:T(8,128)(2,1)}, u32[]{:S(2)}, u32[]{:S(2)}) collective-permute-start(bf16[256,2048]{1,0:T(8,128)(2,1)} %slice_bitcast_fusion.6.refs_0_), channel_id=1, source_target_pairs={{0,8},{8,0},{16,24},{24,16},{1,9},{9,1},{17,25},{25,17},{2,10},{10... | collective-permute-start | bytes 3145736 | tf_op jit(solution)/shard_map/ppermute | solution.py:27
  1312.6 47.5 %collective-permute-start.199 = (bf16[272,2048]{1,0:T(8,128)(2,1)S(1)}, bf16[272,2048]{1,0:T(8,128)(2,1)}, u32[]{:S(2)}, u32[]{:S(2)}) collective-permute-start(bf16[272,2048]{1,0:T(8,128)(2,1)S(1)} %copy-done.60), channel_id=1, source_target_pairs={{0,8},{8,0},{16,24},{24,16},{1,9},{9,1},{17,25},{25,17},{2,10},{10... | collective-permute-start | bytes 3342344 | tf_op jit(solution)/shard_map/ppermute | solution.py:27
  1323.4 59.9 %collective-permute-start.203 = (bf16[272,2048]{1,0:T(8,128)(2,1)}, bf16[272,2048]{1,0:T(8,128)(2,1)}, u32[]{:S(2)}, u32[]{:S(2)}) collective-permute-start(bf16[272,2048]{1,0:T(8,128)(2,1)} %collective-permute-done.201.refs_5_), channel_id=1, source_target_pairs={{0,8},{8,0},{16,24},{24,16},{1,9},{9,1},{17,25},{25,17},{2,10},{10... | collective-permute-start | bytes 3342344 | tf_op jit(solution)/shard_map/ppermute | solution.py:27
  1324.9 32.8 %collective-permute-start.200 = (bf16[256,2048]{1,0:T(8,128)(2,1)}, bf16[256,2048]{1,0:T(8,128)(2,1)}, u32[]{:S(2)}, u32[]{:S(2)}) collective-permute-start(bf16[256,2048]{1,0:T(8,128)(2,1)} %slice_bitcast_fusion.6.refs_0_), channel_id=1, source_target_pairs={{0,16},{8,24},{16,0},{24,8},{1,17},{9,25},{17,1},{25,9},{2,18},{10... | collective-permute-start | bytes 3145736 | tf_op jit(solution)/shard_map/ppermute | solution.py:27
  1335.4 43.1 %collective-permute-start.202 = (bf16[256,2048]{1,0:T(8,128)(2,1)}, bf16[256,2048]{1,0:T(8,128)(2,1)}, u32[]{:S(2)}, u32[]{:S(2)}) collective-permute-start(bf16[256,2048]{1,0:T(8,128)(2,1)} %collective-permute-done.198.refs_2_), channel_id=1, source_target_pairs={{0,16},{8,24},{16,0},{24,8},{1,17},{9,25},{17,1},{25,9},{2,18},{10... | collective-permute-start | bytes 3145736 | tf_op jit(solution)/shard_map/ppermute | solution.py:27
  1353.3 39.7 %collective-permute-start.207 = (f32[8,2048]{1,0:T(8,128)S(1)}, f32[8,2048]{1,0:T(8,128)S(1)}, u32[]{:S(2)}, u32[]{:S(2)}) collective-permute-start(f32[8,2048]{1,0:T(8,128)S(1)} %add.824), channel_id=1, source_target_pairs={{0,8},{8,0},{16,24},{24,16},{1,9},{9,1},{17,25},{25,17},{2,10},{10... | collective-permute-start | bytes 196616 | tf_op jit(solution)/shard_map/ppermute | solution.py:27
  (420 other events, 6070.7 us)
Sparse Core Ops, SparseCore 0:
  19.6 66.1 all-gather.14
  87.4 27.6 all-gather.16
  116.7 105.7 all-gather.18
  223.9 58.0 all-gather.20
  283.4 79.4 all-gather.22
  364.8 105.2 all-gather.24
  476.6 60.3 all-gather.26
  767.5 150.1 reduce-scatter.4
  940.3 77.8 reduce-scatter.6
  1052.8 149.9 reduce-scatter.8
  1228.3 78.8 reduce-scatter.10
